TPU v7x, 32 devices: a whole 2x2x4 slice. The times are simulated.
32 devices in a mesh: dp: 4 (over x, core), pts: 8 (over z, y).
Axes of the slice: x: 2, y: 2, z: 4, core: 2. Of those that a mesh axis runs over, the one named last changes fastest.
Arguments:
- samples_in: float32 [64, 2, 2048], P('dp', None, 'pts'), may hold values from -6 to 6, as said below
- target: float32 [64, 2048], P('dp', 'pts'), may hold values from -6 to 6
- mask: int32 [64, 2048], P('dp', 'pts'), may hold values from 0 to 1
- attn_w: float32 [2, 128, 512], replicated, may hold values from -0.5 to 0.5
- ffn_w: float32 [2, 2, 128, 256], replicated, may hold values from -0.5 to 0.5
- spec_w: float32 [2, 16, 2, 64, 64], replicated, may hold values from -0.5 to 0.5
- dense_w: float32 [320, 64], replicated, may hold values from -0.5 to 0.5
- vectors: float32 [1984], replicated, may hold values from -4 to 4, as said below
- attn_m: float32 [2, 128, 512], replicated
- ffn_m: float32 [2, 2, 128, 256], replicated
- spec_m: float32 [2, 16, 2, 64, 64], replicated
- dense_m: float32 [320, 64], replicated
- vector_m: float32 [1984], replicated
- attn_v: float32 [2, 128, 512], replicated, as said below
- ffn_v: float32 [2, 2, 128, 256], replicated, as said below
- spec_v: float32 [2, 16, 2, 64, 64], replicated, as said below
- dense_v: float32 [320, 64], replicated, as said below
- vector_v: float32 [1984], replicated, as said below
Outputs:
- loss_sum: float32 [], replicated
- valid_count: float32 [], replicated
- attn_m_new: float32 [2, 128, 512], replicated
- attn_v_new: float32 [2, 128, 512], replicated
- attn_w_new: float32 [2, 128, 512], replicated
- attn_w_low: bfloat16 [2, 128, 512], replicated
- ffn_m_new: float32 [2, 2, 128, 256], replicated
- ffn_v_new: float32 [2, 2, 128, 256], replicated
- ffn_w_new: float32 [2, 2, 128, 256], replicated
- ffn_w_low: bfloat16 [2, 2, 128, 256], replicated
- spec_m_new: float32 [2, 16, 2, 64, 64], replicated
- spec_v_new: float32 [2, 16, 2, 64, 64], replicated
- spec_w_new: float32 [2, 16, 2, 64, 64], replicated
- spec_w_low: bfloat16 [2, 16, 2, 64, 64], replicated
- dense_m_new: float32 [320, 64], replicated
- dense_v_new: float32 [320, 64], replicated
- dense_w_new: float32 [320, 64], replicated
- dense_w_low: bfloat16 [320, 64], replicated
- vector_m_new: float32 [1984], replicated
- vector_v_new: float32 [1984], replicated
- vector_w_new: float32 [1984], replicated
- vector_w_low: bfloat16 [1984], replicated
- weight_norms: float32 [8], replicated
- update_norms: float32 [8], replicated
- trust_ratios: float32 [8], replicated
Inputs may be any that keep to these rules, and one draw needn't show every extreme that they name: `samples_in`: row 1 holds the grid points' coordinates, rising by about 1 / 2048 from point to point. `vectors`: the norm gains are positive. `attn_v`: Positive. `ffn_v`: Positive. `spec_v`: Positive. `dense_v`: Positive. `vector_v`: Positive.
All inputs are finite; a program needn't handle non-finite values.
Results may differ from a plain program's by a relative error of at most 0.001.
Values sent between devices are 32-bit elements; how exact they have to be, the bound alone decides.
A program may use at most 192 MiB of HBM per device.

v0:
```python
import math

import jax
import jax.numpy as jnp
from jax import lax
from jax.sharding import PartitionSpec as P

D = 128
HEADS = 4
FF = 256
FREQ = 64
MODES = 16
LAYERS = 2
FLAYERS = 2
STEP = 5


HIGH = lax.Precision.HIGHEST
NORM_EPS = 1e-05
BETA_ONE = 0.5
BETA_TWO = 0.5
RATE = 0.2
DECAY = 0.01
ADAM_EPS = 1e-06


def vector_table():
    entries = [("lift_value", 0, D), ("lift_coord", 0, D), ("lift_bias", 0, D)]
    for layer in range(LAYERS):
        entries = entries + [
            ("key_gain", layer, D),
            ("value_gain", layer, D),
            ("inner_bias", layer, FF),
            ("outer_bias", layer, D),
        ]
    entries = entries + [("proj_bias", 0, FREQ)]
    for layer in range(FLAYERS):
        entries = entries + [("fourier_bias", layer, FREQ)]
    entries = entries + [("head_bias", 0, FREQ), ("head_out", 0, FREQ)]
    offsets = {}
    start = 0
    for label, layer, length in entries:
        offsets[label, layer] = (start, length)
        start = start + length
    return offsets


def pick(vectors, label, layer):
    start, length = vector_table()[label, layer]
    return vectors[start : start + length]


def head_norm(values, gain):
    centred = values - jnp.mean(values, -1, keepdims=True)
    scaled = centred * lax.rsqrt(jnp.mean(centred * centred, -1, keepdims=True) + NORM_EPS)
    return scaled * gain.reshape(HEADS, D // HEADS)


def lift(params, inputs):
    vectors = params[4]
    value = inputs[..., 0, :, None]
    coord = inputs[..., 1, :, None]
    return (
        value * pick(vectors, "lift_value", 0)
        + coord * pick(vectors, "lift_coord", 0)
        + pick(vectors, "lift_bias", 0)
    )


def attn_front(params, rows, layer, points):
    weight = params[0][layer]
    vectors = params[4]
    mixed = jnp.einsum("...d,de->...e", rows, weight[:, : 3 * D], precision=HIGH)
    shape = rows.shape[:-1] + (HEADS, D // HEADS)
    query = mixed[..., :D].reshape(shape)
    keys = head_norm(mixed[..., D : 2 * D].reshape(shape), pick(vectors, "key_gain", layer))
    values = head_norm(mixed[..., 2 * D :].reshape(shape), pick(vectors, "value_gain", layer))
    partial_sum = jnp.einsum("...phe,...phf->...hef", keys, values, precision=HIGH) / points
    return (query, partial_sum)


def attn_rear(params, rows, query, summary, layer):
    weight = params[0][layer]
    attended = jnp.einsum("...phe,...hef->...phf", query, summary, precision=HIGH).reshape(
        rows.shape
    )
    return rows + jnp.einsum("...d,de->...e", attended, weight[:, 3 * D :], precision=HIGH)


def ffn_block(params, rows, layer):
    weight = params[1][layer]
    vectors = params[4]
    inner = jnp.einsum("...d,df->...f", rows, weight[0], precision=HIGH) + pick(
        vectors, "inner_bias", layer
    )
    outer = jnp.einsum("...f,df->...d", jax.nn.gelu(inner), weight[1], precision=HIGH)
    return rows + outer + pick(vectors, "outer_bias", layer)


def project(params, rows):
    return jnp.einsum("...d,df->...f", rows, params[3][:D], precision=HIGH) + pick(
        params[4], "proj_bias", 0
    )


def mode_table(count, total):
    position = jnp.arange(count, dtype=jnp.int32)
    orders = jnp.arange(MODES, dtype=jnp.int32)
    phase = orders[:, None] * position[None, :] % total
    angle = phase.astype(jnp.float32) * (2.0 * math.pi / total)
    return jnp.concatenate([jnp.cos(angle), jnp.sin(angle)], 0)


def spectral_mix(coef, spec, first, width):
    columns = lax.dynamic_slice_in_dim(spec, first, width, 3)
    cosine = coef[..., :MODES, :]
    sine = coef[..., MODES:, :]
    real_part = columns[:, 0]
    imag_part = columns[:, 1]
    mixed_cos = jnp.einsum("...mf,mfg->...mg", cosine, real_part, precision=HIGH) + jnp.einsum(
        "...mf,mfg->...mg", sine, imag_part, precision=HIGH
    )
    mixed_sin = jnp.einsum("...mf,mfg->...mg", sine, real_part, precision=HIGH) - jnp.einsum(
        "...mf,mfg->...mg", cosine, imag_part, precision=HIGH
    )
    return jnp.concatenate([mixed_cos, mixed_sin], -2)


def fourier_end(params, back, rows, layer):
    local = params[3][D + layer * FREQ : D + (layer + 1) * FREQ]
    inner = back + jnp.einsum("...f,fg->...g", rows, local, precision=HIGH)
    return jax.nn.gelu(inner + pick(params[4], "fourier_bias", layer))


def head_loss(params, rows, target, mask_f):
    start = D + FLAYERS * FREQ
    hidden = jax.nn.gelu(
        jnp.einsum("...f,fg->...g", rows, params[3][start : start + FREQ], precision=HIGH)
        + pick(params[4], "head_bias", 0)
    )
    pred = jnp.einsum("...f,f->...", hidden, pick(params[4], "head_out", 0), precision=HIGH)
    diff = pred - target
    return jnp.sum(mask_f * diff * diff)


def add_all(first, second):
    return jax.tree.map(jnp.add, first, second)


def spectral_setup(points, parts):
    width = FREQ // parts
    return (mode_table(points, points), lax.axis_index("pts") * width, width, points)


def fourier_mix(spec, field, setup):
    grid, column, width, points = setup
    channel_rows = lax.all_to_all(field, "pts", split_axis=2, concat_axis=1, tiled=True)
    own_coef = jnp.einsum("kp,spc->skc", grid, channel_rows, precision=HIGH) / math.sqrt(points)
    full = lax.all_gather(own_coef, "pts", axis=2, tiled=True)
    mixed = spectral_mix(full, spec, column, width)
    spread = jnp.einsum("kp,skc->spc", grid, mixed, precision=HIGH) / math.sqrt(MODES)
    back = lax.all_to_all(spread, "pts", split_axis=1, concat_axis=2, tiled=True)
    return (back, full)


def fourier_back(params, grad_out, kept_item, layer, setup):
    field, full, back = kept_item
    grid, column, width, points = setup
    _, end_pull = jax.vjp(
        lambda weights, spread, inner: fourier_end(weights, spread, inner, layer),
        params,
        back,
        field,
    )
    grads, grad_back, grad_field = end_pull(grad_out)
    _, mix_pull = jax.vjp(
        lambda coef, weight: spectral_mix(coef, weight, column, width), full, params[2][layer]
    )
    grad_rows = lax.all_to_all(grad_back, "pts", split_axis=2, concat_axis=1, tiled=True)
    grad_mixed = jnp.einsum("kp,spc->skc", grid, grad_rows, precision=HIGH) / math.sqrt(MODES)
    grad_full, grad_spec = mix_pull(grad_mixed)
    grad_coef = lax.psum_scatter(grad_full, "pts", scatter_dimension=2, tiled=True)
    grad_chan = jnp.einsum("kp,skc->spc", grid, grad_coef, precision=HIGH) / math.sqrt(points)
    grad_field = grad_field + lax.all_to_all(
        grad_chan, "pts", split_axis=1, concat_axis=2, tiled=True
    )
    grads = (grads[0], grads[1], grads[2].at[layer].add(grad_spec), grads[3], grads[4])
    return (grads, grad_field)


def attention_back(params, grad_rows, kept_item, layer, points):
    rows, summary = kept_item
    (query, partial_sum), front_pull = jax.vjp(
        lambda weights, inner: attn_front(weights, inner, layer, points), params, rows
    )
    summary = lax.psum(partial_sum, "pts")
    middle, rear_pull = jax.vjp(
        lambda weights, inner, asked, summed: attn_rear(weights, inner, asked, summed, layer),
        params,
        rows,
        query,
        summary,
    )
    _, ffn_pull = jax.vjp(lambda weights, inner: ffn_block(weights, inner, layer), params, middle)
    ffn_grads, grad_middle = ffn_pull(grad_rows)
    rear_grads, grad_direct, grad_query, grad_summary = rear_pull(grad_middle)
    grad_summary = lax.psum(grad_summary, "pts")
    front_grads, grad_front = front_pull((grad_query, grad_summary))
    return (add_all(add_all(ffn_grads, rear_grads), front_grads), grad_direct + grad_front)


def lamb(weight, grad, first, second):
    first_new = BETA_ONE * first + (1.0 - BETA_ONE) * grad
    second_new = BETA_TWO * second + (1.0 - BETA_TWO) * grad * grad
    update = (
        first_new
        / (1.0 - BETA_ONE**STEP)
        / (jnp.sqrt(second_new / (1.0 - BETA_TWO**STEP)) + ADAM_EPS)
        + DECAY * weight
    )
    return (first_new, second_new, update)


def trust_step(weight, update, stacked):
    axes = tuple(range(1, weight.ndim)) if stacked else tuple(range(weight.ndim))
    weight_norm = jnp.sqrt(jnp.sum(weight * weight, axes))
    update_norm = jnp.sqrt(jnp.sum(update * update, axes))
    ratio = weight_norm / (update_norm + ADAM_EPS)
    scale = ratio.reshape(ratio.shape + (1,) * (weight.ndim - ratio.ndim))
    return (
        weight - RATE * scale * update,
        jnp.atleast_1d(weight_norm),
        jnp.atleast_1d(update_norm),
        jnp.atleast_1d(ratio),
    )


def finish(loss_sum, valid_count, params, grads, firsts, seconds):
    results = [loss_sum, valid_count]
    weight_norms, update_norms, ratios = ([], [], [])
    for weight, grad, first, second, stacked in zip(
        params, grads, firsts, seconds, (True, True, True, False, False)
    ):
        first_new, second_new, update = lamb(weight, grad, first, second)
        fresh, weight_norm, update_norm, ratio = trust_step(weight, update, stacked)
        results = results + [first_new, second_new, fresh, fresh.astype(jnp.bfloat16)]
        weight_norms.append(weight_norm)
        update_norms.append(update_norm)
        ratios.append(ratio)
    return results + [
        jnp.concatenate(weight_norms),
        jnp.concatenate(update_norms),
        jnp.concatenate(ratios),
    ]


def body(
    samples_in,
    target,
    mask,
    attn_w,
    ffn_w,
    spec_w,
    dense_w,
    vectors,
    attn_m,
    ffn_m,
    spec_m,
    dense_m,
    vector_m,
    attn_v,
    ffn_v,
    spec_v,
    dense_v,
    vector_v,
):
    params = (attn_w, ffn_w, spec_w, dense_w, vectors)
    parts = lax.axis_size("pts")
    local_pts = samples_in.shape[2]
    points = local_pts * parts
    mask_f = mask.astype(jnp.float32)
    valid_count = lax.psum(jnp.sum(mask_f), ("dp", "pts"))
    setup = spectral_setup(points, parts)
    rows, lift_pull = jax.vjp(lambda weights: lift(weights, samples_in), params)
    kept = []
    for layer in range(LAYERS):
        query, partial_sum = attn_front(params, rows, layer, points)
        summary = lax.psum(partial_sum, "pts")
        kept.append((rows, summary))
        rows = ffn_block(params, attn_rear(params, rows, query, summary, layer), layer)
    field, proj_pull = jax.vjp(project, params, rows)
    spectral_kept = []
    for layer in range(FLAYERS):
        back, full = fourier_mix(params[2][layer], field, setup)
        spectral_kept.append((field, full, back))
        field = fourier_end(params, back, field, layer)
    loss_part, head_pull = jax.vjp(
        lambda weights, inner: head_loss(weights, inner, target, mask_f), params, field
    )
    grads, grad_field = head_pull(1.0 / valid_count)
    for layer in reversed(range(FLAYERS)):
        layer_grads, grad_field = fourier_back(
            params, grad_field, spectral_kept[layer], layer, setup
        )
        grads = add_all(grads, layer_grads)
    proj_grads, grad_rows = proj_pull(grad_field)
    grads = add_all(grads, proj_grads)
    for layer in reversed(range(LAYERS)):
        layer_grads, grad_rows = attention_back(params, grad_rows, kept[layer], layer, points)
        grads = add_all(grads, layer_grads)
    grads = add_all(grads, lift_pull(grad_rows)[0])
    summed = lax.psum((grads[0], grads[1], grads[2], grads[3], grads[4], loss_part), ("dp", "pts"))
    out = finish(
        summed[5],
        valid_count,
        params,
        summed[:5],
        (attn_m, ffn_m, spec_m, dense_m, vector_m),
        (attn_v, ffn_v, spec_v, dense_v, vector_v),
    )
    return (
        out[0],
        out[1],
        out[2],
        out[3],
        out[4],
        out[5],
        out[6],
        out[7],
        out[8],
        out[9],
        out[10],
        out[11],
        out[12],
        out[13],
        out[14],
        out[15],
        out[16],
        out[17],
        out[18],
        out[19],
        out[20],
        out[21],
        out[22],
        out[23],
        out[24],
    )


def solution(mesh):
    placed = (
        P("dp", None, "pts"),
        P("dp", "pts"),
        P("dp", "pts"),
        P(),
        P(),
        P(),
        P(),
        P(),
        P(),
        P(),
        P(),
        P(),
        P(),
        P(),
        P(),
        P(),
        P(),
        P(),
    )
    return jax.shard_map(
        body,
        mesh=mesh,
        in_specs=placed,
        out_specs=(
            P(),
            P(),
            P(),
            P(),
            P(),
            P(),
            P(),
            P(),
            P(),
            P(),
            P(),
            P(),
            P(),
            P(),
            P(),
            P(),
            P(),
            P(),
            P(),
            P(),
            P(),
            P(),
            P(),
            P(),
            P(),
        ),
        check_vma=False,
    )
```

profile of v0, /device:TPU:0, one launch (start us, length us, event | category | flops | bytes accessed | tf_op | source)
XLA Modules:
  0.0 1401.9 jit_solution(6525497972184997277)
XLA Ops:
  38.5 78.4 %all-reduce.56.cloned.1.call-done = f32[16,4,32,32]{3,2,1,0:T(8,128)} async-done(((f32[16,4,32,32]{3,2,1,0:T(8,128)}), f32[16,4,32,32]{3,2,1,0:T(8,128)}) %all-reduce.56.cloned.1.call-update) | async-done | bytes 262160 | tf_op jit(solution)/shard_map/psum | solution.py:288
  128.3 14.3 %add_add_fusion.5 = f32[16,256,128]{2,1,0:T(8,128)S(1)} fusion(f32[16,256,128]{2,1,0:T(8,128)S(1)} %fusion.25, f32[16,256,256]{2,1,0:T(8,128)S(1)} %fusion.152, f32[256]{0:T(256)S(1)} %get-tuple-element.151, f32[128]{0:T(128)S(1)} %get-tuple-element.144, f32[2,2,128,256]{3,2,1,0:T(8,128)S(1)} %copy-done.41), kind=kOutput, calls=%fused_computation.73 | convolution fusion | flops 1621098496 | bytes 8521216 | tf_op jit(solution)/shard_map/...f,df->...d/dot_general | solution.py:96
  173.0 73.8 %all-reduce.58.cloned.1.call-done = f32[16,4,32,32]{3,2,1,0:T(8,128)} async-done(((f32[16,4,32,32]{3,2,1,0:T(8,128)}), f32[16,4,32,32]{3,2,1,0:T(8,128)}) %all-reduce.58.cloned.1.call-update) | async-done | bytes 262160 | tf_op jit(solution)/shard_map/psum | solution.py:288
  279.4 19.2 %all-to-all-done = f32[16,256,64]{1,0,2:T(8,128)} async-done(((f32[16,256,64]{1,0,2:T(8,128)}), f32[16,256,64]{1,0,2:T(8,128)}, u32[]{:S(2)}, u32[]{:S(2)}) %all-to-all-start) | async-done | bytes 1048608 | tf_op jit(solution)/shard_map/all_to_all | solution.py:157
  301.4 31.6 %all_gather.6 = f32[16,32,64]{1,2,0:T(8,128)S(1)} all-gather(f32[16,32,8]{1,2,0:T(8,128)S(1)} %fusion.84), channel_id=1, replica_groups=mesh['dp'=4,'pts'=8] {'pts'}, dimensions={2}, use_global_device_ids=true | all-gather | bytes 147456 | tf_op jit(solution)/shard_map/all_gather | solution.py:159
  353.3 8.1 reshape.502
  361.4 23.9 %all_to_all.144 = f32[8,1,32768]{2,1,0:T(1,128)} all-to-all(f32[8,1,32768]{2,1,0:T(1,128)} %reshape.502), channel_id=1, replica_groups=mesh['dp'=4,'pts'=8] {'pts'}, dimensions={0} | all-to-all | bytes 2097152 | tf_op jit(solution)/shard_map/all_to_all | solution.py:162
  391.1 7.3 reshape.503
  416.3 20.6 %all-to-all-done.2 = f32[16,256,64]{1,0,2:T(8,128)} async-done(((f32[16,256,64]{1,0,2:T(8,128)}), f32[16,256,64]{1,0,2:T(8,128)}, u32[]{:S(2)}, u32[]{:S(2)}) %all-to-all-start.2) | async-done | bytes 1048608 | tf_op jit(solution)/shard_map/all_to_all | solution.py:157
  439.7 31.7 %all_gather.7 = f32[16,32,64]{1,2,0:T(8,128)S(1)} all-gather(f32[16,32,8]{1,2,0:T(8,128)S(1)} %fusion.83), channel_id=1, replica_groups=mesh['dp'=4,'pts'=8] {'pts'}, dimensions={2}, use_global_device_ids=true | all-gather | bytes 147456 | tf_op jit(solution)/shard_map/all_gather | solution.py:159
  492.6 8.1 reshape.504
  500.7 22.0 %all_to_all.145 = f32[8,1,32768]{2,1,0:T(1,128)} all-to-all(f32[8,1,32768]{2,1,0:T(1,128)} %reshape.504), channel_id=1, replica_groups=mesh['dp'=4,'pts'=8] {'pts'}, dimensions={0} | all-to-all | bytes 2097152 | tf_op jit(solution)/shard_map/all_to_all | solution.py:162
  528.1 7.3 reshape.505
  548.4 39.2 %psum.86 = f32[]{:T(128)} all-reduce(f32[]{:T(128)} %get-tuple-element.68), channel_id=1, replica_groups=mesh['dp'=4,'pts'=8] {'dp','pts'}, use_global_device_ids=true, to_apply=%region_13.14 | all-reduce | flops 1 | bytes 8 | tf_op jit(solution)/shard_map/psum | solution.py:282
  595.4 29.5 %all_to_all.146 = f32[16,256,64]{1,0,2:T(8,128)S(1)} all-to-all(f32[16,256,64]{1,0,2:T(8,128)S(1)} %copy.256), channel_id=1, replica_groups=mesh['dp'=4,'pts'=8] {'pts'}, dimensions={2} | all-to-all | bytes 2097152 | tf_op jit(solution)/shard_map/all_to_all | solution.py:179
  639.9 60.5 %reduce-scatter.3.cloned.1.call-done = f32[16,32,8]{1,0,2:T(8,128)} async-done(((f32[16,32,64]{1,0,2:T(8,128)}), f32[16,32,8]{1,0,2:T(8,128)}) %reduce-scatter.3.cloned.1.call-update) | async-done | bytes 16400 | tf_op jit(solution)/shard_map/reduce_scatter | solution.py:182
  709.4 8.1 reshape.506
  717.5 28.6 %all_to_all.147 = f32[8,1,32768]{2,1,0:T(1,128)} all-to-all(f32[8,1,32768]{2,1,0:T(1,128)} %reshape.506), channel_id=1, replica_groups=mesh['dp'=4,'pts'=8] {'pts'}, dimensions={0} | all-to-all | bytes 2097152 | tf_op jit(solution)/shard_map/all_to_all | solution.py:184
  751.4 7.3 reshape.507
  769.8 28.7 %all_to_all.148 = f32[16,256,64]{1,0,2:T(8,128)S(1)} all-to-all(f32[16,256,64]{1,0,2:T(8,128)S(1)} %copy.267), channel_id=1, replica_groups=mesh['dp'=4,'pts'=8] {'pts'}, dimensions={2} | all-to-all | bytes 2097152 | tf_op jit(solution)/shard_map/all_to_all | solution.py:179
  819.2 55.3 %reduce-scatter.5.cloned.1.call-done = f32[16,32,8]{1,0,2:T(8,128)} async-done(((f32[16,32,64]{1,0,2:T(8,128)}), f32[16,32,8]{1,0,2:T(8,128)}) %reduce-scatter.5.cloned.1.call-update) | async-done | bytes 16400 | tf_op jit(solution)/shard_map/reduce_scatter | solution.py:182
  883.5 8.1 reshape.508
  933.0 6.4 copy.276
  953.1 6.7 fusion.276
  986.6 74.7 %all-reduce.60.cloned.1.call-done = f32[16,4,32,32]{3,2,1,0:T(8,128)} async-done(((f32[16,4,32,32]{3,2,1,0:T(8,128)}), f32[16,4,32,32]{3,2,1,0:T(8,128)}) %all-reduce.60.cloned.1.call-update) | async-done | bytes 262160 | tf_op jit(solution)/shard_map/psum | solution.py:207
  1085.0 7.1 fusion.66
  1103.5 6.7 fusion.274
  1136.5 66.4 %all-reduce.62.cloned.1.call-done = f32[16,4,32,32]{3,2,1,0:T(8,128)} async-done(((f32[16,4,32,32]{3,2,1,0:T(8,128)}), f32[16,4,32,32]{3,2,1,0:T(8,128)}) %all-reduce.62.cloned.1.call-update) | async-done | bytes 262160 | tf_op jit(solution)/shard_map/psum | solution.py:207
  1226.7 8.1 fusion.65
  1241.8 7.5 fusion.252
  1249.6 40.4 %all-reduce.48 = (f32[]{:T(128)}, f32[1984]{0:T(1024)S(1)}) all-reduce(f32[]{:T(128)} %get-tuple-element.69, f32[1984]{0:T(1024)S(1)} %add_add_fusion.12), channel_id=1, replica_groups=mesh['dp'=4,'pts'=8] {'dp','pts'}, use_global_device_ids=true, to_apply=%region_11.12 | all-reduce | flops 1985 | bytes 15880 | tf_op jit(solution)/shard_map/psum | solution.py:312
  1293.4 81.9 %all-reduce.64.cloned.1.call-done = (f32[2,128,512]{2,1,0:T(8,128)}, f32[2,2,128,256]{3,2,1,0:T(8,128)}, f32[2,16,2,64,64]{4,3,2,1,0:T(8,128)}, f32[320,64]{0,1:T(8,128)}) async-done(((f32[2,128,512]{2,1,0:T(8,128)}, f32[2,2,128,256]{3,2,1,0:T(8,128)}, f32[2,16,2,64,64]{4,3,2,1,0:T(8,128)}, f32[320,64]{0,1:T(8,128)}), (f32[2,128,512]{2,1,0:T(8,128)}, f32[2,2,128,256]{3,2,1,0:T(8,128)}, ...) | async-done | bytes 2179088 | tf_op jit(solution)/shard_map/psum | solution.py:312
  (518 shorter events, 464.3 us)
Async XLA Ops:
  7.2 109.7 %all-reduce.56.cloned.1.call-start = ((), (), s32[]{:S(2)}) async-start(), calls=%async_computation.10 | async-start | bytes 2097152 | tf_op jit(solution)/shard_map/psum | solution.py:288
  8.2 111.9 %copy-start.118 = (f32[128]{0:T(128)}, f32[128]{0:T(128)S(1)}, u32[]{:S(2)}) copy-start(f32[128]{0:T(128)S(1)} %get-tuple-element.147) | copy-start | bytes 1540
  8.2 111.9 %copy-start.119 = (f32[128]{0:T(128)}, f32[128]{0:T(128)S(1)}, u32[]{:S(2)}) copy-start(f32[128]{0:T(128)S(1)} %get-tuple-element.148) | copy-start | bytes 1540
  8.2 111.9 %copy-start.120 = (f32[128]{0:T(128)}, f32[128]{0:T(128)S(1)}, u32[]{:S(2)}) copy-start(f32[128]{0:T(128)S(1)} %get-tuple-element.149) | copy-start | bytes 1540
  10.3 109.8 %copy-start.72 = (f32[128,512]{1,0:T(8,128)}, f32[128,512]{1,0:T(8,128)S(1)}, u32[]{:S(2)}) copy-start(f32[128,512]{1,0:T(8,128)S(1)} %get-tuple-element.127) | copy-start | bytes 786436
  10.3 240.5 %copy-start.54 = (f32[128,512]{1,0:T(8,128)}, f32[128,512]{1,0:T(8,128)S(1)}, u32[]{:S(2)}) copy-start(f32[128,512]{1,0:T(8,128)S(1)} %get-tuple-element.126) | copy-start | bytes 786436
  10.3 109.8 %copy-start.96 = (f32[16,256]{1,0:T(8,128)}, f32[16,256]{1,0:T(8,128)S(1)}, u32[]{:S(2)}) copy-start(f32[16,256]{1,0:T(8,128)S(1)} %get-tuple-element.182) | copy-start | bytes 49156
  10.3 109.8 %copy-start.98 = (f32[16,256]{1,0:T(8,128)}, f32[16,256]{1,0:T(8,128)S(1)}, u32[]{:S(2)}) copy-start(f32[16,256]{1,0:T(8,128)S(1)} %get-tuple-element.183) | copy-start | bytes 49156
  36.1 210.8 %all-reduce.58.cloned.1.call-start = ((), (), s32[]{:S(2)}) async-start(), calls=%async_computation.11 | async-start | bytes 2097152 | tf_op jit(solution)/shard_map/psum | solution.py:288
  38.5 81.6 %copy-start.19 = (f32[16,256,128]{1,2,0:T(8,128)}, f32[16,256,128]{1,2,0:T(8,128)S(1)}, u32[]{:S(2)}) copy-start(f32[16,256,128]{1,2,0:T(8,128)S(1)} %copy.228) | copy-start | bytes 6291460
  38.5 89.7 %copy-start.131 = (f32[256]{0:T(256)}, f32[256]{0:T(256)S(1)}, u32[]{:S(2)}) copy-start(f32[256]{0:T(256)S(1)} %get-tuple-element.151) | copy-start | bytes 3076
  38.5 219.5 %copy-start.133 = (f32[256]{0:T(256)}, f32[256]{0:T(256)S(1)}, u32[]{:S(2)}) copy-start(f32[256]{0:T(256)S(1)} %get-tuple-element.150) | copy-start | bytes 3076
  268.8 29.8 %all-to-all-start = ((f32[16,256,64]{1,0,2:T(8,128)}), f32[16,256,64]{1,0,2:T(8,128)}, u32[]{:S(2)}, u32[]{:S(2)}) async-start(f32[16,256,64]{1,0,2:T(8,128)} %copy.236), calls=%async_computation | async-start | bytes 2097152 | tf_op jit(solution)/shard_map/all_to_all | solution.py:157
  409.8 27.2 %all-to-all-start.2 = ((f32[16,256,64]{1,0,2:T(8,128)}), f32[16,256,64]{1,0,2:T(8,128)}, u32[]{:S(2)}, u32[]{:S(2)}) async-start(f32[16,256,64]{1,0,2:T(8,128)} %copy.245), calls=%async_computation.2 | async-start | bytes 2097152 | tf_op jit(solution)/shard_map/all_to_all | solution.py:157
  414.0 286.4 %reduce-scatter.3.cloned.1.call-start = ((), (), s32[]{:S(2)}) async-start(), calls=%async_computation.12 | async-start | bytes 589824 | tf_op jit(solution)/shard_map/reduce_scatter | solution.py:182
  639.9 234.7 %reduce-scatter.5.cloned.1.call-start = ((), (), s32[]{:S(2)}) async-start(), calls=%async_computation.13 | async-start | bytes 589824 | tf_op jit(solution)/shard_map/reduce_scatter | solution.py:182
  891.6 31.0 %all-to-all-start.7 = ((f32[8,1,32768]{2,1,0:T(1,128)}), f32[8,1,32768]{2,1,0:T(1,128)}, u32[]{:S(2)}, u32[]{:S(2)}) async-start(f32[8,1,32768]{2,1,0:T(1,128)} %reshape.508), calls=%async_computation.9 | async-start | bytes 2097152 | tf_op jit(solution)/shard_map/all_to_all | solution.py:184
  896.0 165.4 %all-reduce.60.cloned.1.call-start = ((), (), s32[]{:S(2)}) async-start(), calls=%async_computation.14 | async-start | bytes 2097152 | tf_op jit(solution)/shard_map/psum | solution.py:207
  976.2 226.7 %all-reduce.62.cloned.1.call-start = ((), (), s32[]{:S(2)}) async-start(), calls=%async_computation.15 | async-start | bytes 2097152 | tf_op jit(solution)/shard_map/psum | solution.py:207
  982.1 79.2 %copy-start.68 = (f32[16,256,4]{1,2,0:T(4,128)S(1)}, f32[16,256,4]{1,2,0:T(4,128)}, u32[]{:S(2)}) copy-start(f32[16,256,4]{1,2,0:T(4,128)} %copy-done.67) | copy-start | bytes 196612
  986.6 79.2 %copy-start.90 = (f32[16,256,4]{1,2,0:T(4,128)S(1)}, f32[16,256,4]{1,2,0:T(4,128)}, u32[]{:S(2)}) copy-start(f32[16,256,4]{1,2,0:T(4,128)} %copy-done.89) | copy-start | bytes 196612
  986.6 79.3 %copy-start.70 = (f32[16,256,4]{1,2,0:T(4,128)S(1)}, f32[16,256,4]{1,2,0:T(4,128)}, u32[]{:S(2)}) copy-start(f32[16,256,4]{1,2,0:T(4,128)} %copy-done.69) | copy-start | bytes 196612
  1125.0 250.3 %all-reduce.64.cloned.1.call-start = ((), (), s32[]{:S(2)}) async-start(), calls=%async_computation.16 | async-start | bytes 6488064 | tf_op jit(solution)/shard_map/psum | solution.py:312
  1130.3 72.6 %copy-start.1 = (f32[16,256,4,32]{1,3,2,0:T(8,128)S(1)}, f32[16,256,4,32]{1,3,2,0:T(8,128)}, u32[]{:S(2)}) copy-start(f32[16,256,4,32]{1,3,2,0:T(8,128)} %copy-done) | copy-start | bytes 6291460
  1130.3 72.6 %copy-start.64 = (f32[16,256,4]{1,2,0:T(4,128)S(1)}, f32[16,256,4]{1,2,0:T(4,128)}, u32[]{:S(2)}) copy-start(f32[16,256,4]{1,2,0:T(4,128)} %copy-done.63) | copy-start | bytes 196612
  1130.3 72.6 %copy-start.103 = (f32[4,32]{1,0:T(4,128)S(1)}, f32[4,32]{1,0:T(4,128)}, u32[]{:S(2)}) copy-start(f32[4,32]{1,0:T(4,128)} %copy-done.102) | copy-start | bytes 1540
  1130.3 72.6 %copy-start.105 = (f32[4,32]{1,0:T(4,128)S(1)}, f32[4,32]{1,0:T(4,128)}, u32[]{:S(2)}) copy-start(f32[4,32]{1,0:T(4,128)} %copy-done.104) | copy-start | bytes 1540
  1136.5 70.9 %copy-start.66 = (f32[16,256,4]{1,2,0:T(4,128)S(1)}, f32[16,256,4]{1,2,0:T(4,128)}, u32[]{:S(2)}) copy-start(f32[16,256,4]{1,2,0:T(4,128)} %copy-done.65) | copy-start | bytes 196612
  1241.8 136.6 %copy-start.43 = (f32[2,128,512]{2,1,0:T(8,128)S(1)}, f32[2,128,512]{2,1,0:T(8,128)}, u32[]{:S(2)}) copy-start(f32[2,128,512]{2,1,0:T(8,128)} %param.25) | copy-start | bytes 1572868
  1249.3 131.2 %copy-start.93 = (f32[2,2,128,256]{3,2,1,0:T(8,128)S(1)}, f32[2,2,128,256]{3,2,1,0:T(8,128)}, u32[]{:S(2)}) copy-start(f32[2,2,128,256]{3,2,1,0:T(8,128)} %param.36) | copy-start | bytes 1572868
  1291.3 91.3 %copy-start.113 = (f32[1984]{0:T(1024)}, f32[1984]{0:T(1024)S(1)}, u32[]{:S(2)}) copy-start(f32[1984]{0:T(1024)S(1)} %get-tuple-element.80) | copy-start | bytes 23812
  1291.3 91.4 %copy-start.114 = (f32[1984]{0:T(1024)}, f32[1984]{0:T(1024)S(1)}, u32[]{:S(2)}) copy-start(f32[1984]{0:T(1024)S(1)} %get-tuple-element.81) | copy-start | bytes 23812
  (117 other events, 744.2 us)
Sparse Core Ops, SparseCore 0:
  36.2 80.6 all-reduce.55
  169.3 77.5 all-reduce.57
  640.0 60.3 reduce-scatter.2
  813.6 60.9 reduce-scatter.4
  976.3 85.0 all-reduce.59
  1125.1 77.7 all-reduce.61
  1235.9 139.3 all-reduce.63
where the time goes:
time: 1410 us; the launch traced here: 1400 us
  waiting for transfers between devices  531 us (38%)
  blocking collectives  276 us (20%)
  matrix products  249 us (18%)
  local copies, waits for them, and re-layouts  228 us (16%)
  other arithmetic  84 us (6%)
  between operations  20.1 us (1%)
    psum x2, waiting for transfers between devices, body(): summary = lax.psum(partial_sum, 'pts')  152 us
    psum x2, waiting for transfers between devices, attention_back(): grad_summary = lax.psum(grad_summary, 'pts')  141 us
    reduce_scatter x2, waiting for transfers between devices, fourier_back(): lax.psum_scatter(grad_full, 'pts', scatter_dimension=2, tiled=True)  116 us
    psum x1, waiting for transfers between devices, body(): lax.psum((grads[0], grads[1], grads[2], grads[3], grads[4], loss_part), (...  81.9 us
    unnamed x286, local copies, waits for them, and re-layouts  71.2 us
    all_gather x2, blocking collectives, fourier_mix(): full = lax.all_gather(own_coef, 'pts', axis=2, tiled=True)  63.2 us
    all_to_all x2, blocking collectives, fourier_back(): lax.all_to_all(grad_back, 'pts', split_axis=2, concat_axis=1, tiled=True)  58.2 us
    all_to_all x2, blocking collectives, fourier_mix(): lax.all_to_all(spread, 'pts', split_axis=1, concat_axis=2, tiled=True)  45.9 us
  transfers between devices with their start and end apart: 10, of which 9 were waited for; matrix products, arithmetic and copies ran while one was open for 6% of the time, Pallas kernels for 0%

commit v1 on v0

--- a/solution.py
+++ b/solution.py
@@ -2,7 +2,11 @@
 
 import jax
 import jax.numpy as jnp
+import ml_dtypes
+import numpy as np
 from jax import lax
+from jax.experimental import pallas as pl
+from jax.experimental.pallas import tpu as pltpu
 from jax.sharding import PartitionSpec as P
 
 D = 128
@@ -347,6 +351,792 @@
     )
 
 
+F32 = jnp.float32
+BF16 = jnp.bfloat16
+ROWS = 512
+
+
+def dot(first, second, left=1, right=0, precision=None):
+    return lax.dot_general(
+        first,
+        second,
+        (((left,), (right,)), ((), ())),
+        precision=precision,
+        preferred_element_type=F32,
+    )
+
+
+def exact(first, second, left=1, right=0):
+    return dot(first, second, left, right, HIGH)
+
+
+def halves(value):
+    high = value.astype(BF16)
+    return high, (value - high.astype(F32)).astype(BF16)
+
+
+def thirds(value):
+    high = value.astype(BF16)
+    rest = value - high.astype(F32)
+    middle = rest.astype(BF16)
+    return high, middle, (rest - middle.astype(F32)).astype(BF16)
+
+
+def beside(*pieces):
+    return jnp.concatenate(pieces, 1)
+
+
+def above(*pieces):
+    return jnp.concatenate(pieces, 0)
+
+
+def fold(value):
+    half = value.shape[1] // 2
+    return value[:, :half] + value[:, half:]
+
+
+def column_sum(value):
+    rows, width = value.shape
+    return jnp.sum(value.reshape(rows // 8, 8, width), 0)
+
+
+def gelu_pair(inner):
+    scale = math.sqrt(2.0 / math.pi)
+    square = inner * inner
+    bend = jnp.tanh(inner * (scale + (scale * 0.044715) * square))
+    half = 0.5 + 0.5 * bend
+    slope = half + (0.5 * inner) * (1.0 - bend * bend) * (scale + (3.0 * scale * 0.044715) * square)
+    return inner * half, slope
+
+
+def wide6_weight(weight):
+    high, middle, low = thirds(weight)
+    return above(high, high, middle, middle, low, high)
+
+
+def wide6(pieces, weight):
+    high, middle, low = pieces
+    return dot(beside(high, middle, high, middle, high, low), weight)
+
+
+def tall6_weight(weight):
+    high, middle, low = thirds(weight)
+    pair = beside(high, middle)
+    return above(pair, pair), above(low, high)
+
+
+def tall6(pieces, weights):
+    high, middle, low = pieces
+    return fold(dot(beside(high, middle), weights[0])) + dot(beside(high, low), weights[1])
+
+
+def wide4_weight(weight):
+    high, low = halves(weight)
+    return above(high, high, low, low)
+
+
+def wide4(pieces, weight):
+    high, low = pieces
+    return dot(beside(high, low, high, low), weight)
+
+
+def tall4_weight(weight):
+    high, low = halves(weight)
+    pair = beside(high, low)
+    return above(pair, pair)
+
+
+def tall4(pieces, weight):
+    return fold(dot(beside(*pieces), weight))
+
+
+def head_blocks(width):
+    row = lax.broadcasted_iota(jnp.int32, (width, width), 0)
+    column = lax.broadcasted_iota(jnp.int32, (width, width), 1)
+    return row // (D // HEADS) == column // (D // HEADS)
+
+
+def doubled(weight):
+    zero = jnp.zeros_like(weight)
+    return above(beside(weight, zero), beside(zero, weight))
+
+
+def local_kernel(
+    inputs_ref,
+    attn_ref,
+    ffn_ref,
+    spec_ref,
+    dense_ref,
+    vec_ref,
+    table_ref,
+    trow_ref,
+    g_attn,
+    g_ffn,
+    g_spec,
+    g_dense,
+    g_vec,
+    g_loss,
+    lifted,
+    lrows,
+    w_kv,
+    w_kvt,
+    w_in,
+    w_int,
+    w0_u,
+    mid_rows,
+    w_out0,
+    w_out1,
+    w_outt,
+    x_keep,
+    r_keep,
+    slope_keep,
+    act_keep,
+    mid_keep,
+    h1_keep,
+    h2_keep,
+    z_keep,
+    zs_keep,
+    e_keep,
+    s_acc,
+    w0_kv,
+    w0_g,
+    n_keep,
+    small_keep,
+    nt_keep,
+    cent_keep,
+    coef_acc,
+    coef_keep,
+    stack_ref,
+    sq_acc,
+    p_acc,
+    y_acc,
+    w2_acc,
+    w1_acc,
+    kv_acc,
+    v_acc,
+    u_acc,
+    vt_acc,
+    b_acc,
+    d_keep,
+    t_keep,
+    wz,
+):
+    count, points = inputs_ref.shape[0], inputs_ref.shape[2]
+    total = count * points
+    steps = points // ROWS
+    rows_all = total // ROWS
+    blocks = head_blocks(D)
+    block_f = jnp.where(blocks, 1.0, 0.0).astype(F32)
+    block_b = block_f.astype(BF16)
+    mean_weight = above(block_b, block_b)
+    centre = (
+        jnp.where(
+            lax.broadcasted_iota(jnp.int32, (D, D), 0) == lax.broadcasted_iota(jnp.int32, (D, D), 1),
+            1.0,
+            0.0,
+        ).astype(F32)
+        - block_f * (HEADS / D)
+    )
+    eye = jnp.where(
+        lax.broadcasted_iota(jnp.int32, (D, D), 0) == lax.broadcasted_iota(jnp.int32, (D, D), 1), 1.0, 0.0
+    ).astype(F32)
+
+    def vector(label, layer):
+        start, length = vector_table()[label, layer]
+        if length == 2 * D:
+            row = start // D
+            return beside(vec_ref[row : row + 1, :], vec_ref[row + 1 : row + 2, :])
+        row = start // D
+        if length == D:
+            return vec_ref[row : row + 1, :]
+        offset = start - row * D
+        piece = vec_ref[row : row + 1, offset : offset + FREQ]
+        return beside(piece, piece)
+
+    def block(index):
+        return pl.ds(pl.multiple_of(index * ROWS, ROWS), ROWS)
+
+    for s in range(count):
+        data = inputs_ref[s]
+        value, coord, target, valid = data[0:1], data[1:2], data[2:3], data[3:4]
+        one = jnp.ones_like(value)
+        vh, vm, vl = [item.astype(F32) for item in thirds(value)]
+        ch, cm, cl = [item.astype(F32) for item in thirds(coord)]
+        th, tm, tl = [item.astype(F32) for item in thirds(target)]
+        zero = jnp.zeros((D - 19, points), F32)
+        stack = above(vh, vm, vh, vm, vh, vl, ch, cm, ch, cm, ch, cl, one, one, one, th, tm, tl, valid, zero)
+        lifted[s * points : (s + 1) * points, :] = stack.T.astype(BF16)
+        short = above(vh, vm, vl, ch, cm, cl, one, jnp.zeros((9, points), F32)).astype(BF16)
+        for i in range(steps):
+            lrows[s * steps + i] = short[:, i * ROWS : (i + 1) * ROWS]
+
+    lift_rows = above(
+        vector("lift_value", 0), vector("lift_coord", 0), vector("lift_bias", 0), jnp.zeros((5, D), F32)
+    )
+
+    def lift_weight(mixed):
+        high, middle, low = [item.astype(F32) for item in thirds(mixed)]
+        parts = []
+        for i in range(2):
+            hi, mi, lo = high[i : i + 1], middle[i : i + 1], low[i : i + 1]
+            parts += [hi, hi, mi, mi, lo, hi]
+        parts += [high[2:3], middle[2:3], low[2:3]]
+        parts.append(jnp.zeros((D - 15, mixed.shape[1]), F32))
+        return above(*parts).astype(BF16)
+
+    for layer in range(LAYERS):
+        weight = attn_ref[layer]
+        keyed = beside(exact(weight[:, D : 2 * D], centre), exact(weight[:, 2 * D : 3 * D], centre))
+        cent_keep[layer] = keyed
+        if layer == 0:
+            w0_kv[...] = lift_weight(exact(lift_rows, keyed))
+        else:
+            w_kv[...] = wide6_weight(keyed)
+            w_kvt[...] = tall4_weight(keyed.T)
+        first, second = ffn_ref[layer, 0], ffn_ref[layer, 1]
+        if layer:
+            w_in[...] = wide6_weight(first)
+            w_int[...] = tall4_weight(first.T)
+        pair, rest = tall6_weight(second.T)
+        w_out0[layer] = pair
+        w_out1[layer] = rest
+        w_outt[layer] = wide4_weight(second)
+
+    s_acc[...] = jnp.zeros_like(s_acc)
+    coef_acc[...] = jnp.zeros_like(coef_acc)
+    sq_acc[...] = jnp.zeros_like(sq_acc)
+    p_acc[...] = jnp.zeros_like(p_acc)
+    y_acc[...] = jnp.zeros_like(y_acc)
+    w2_acc[...] = jnp.zeros_like(w2_acc)
+    w1_acc[...] = jnp.zeros_like(w1_acc)
+    kv_acc[...] = jnp.zeros_like(kv_acc)
+    v_acc[...] = jnp.zeros_like(v_acc)
+    u_acc[...] = jnp.zeros_like(u_acc)
+    vt_acc[...] = jnp.zeros_like(vt_acc)
+    b_acc[...] = jnp.zeros_like(b_acc)
+
+    def head_scale(centred):
+        high, low = halves(centred * centred)
+        var = beside(
+            dot(beside(high[:, :D], low[:, :D]), mean_weight), dot(beside(high[:, D:], low[:, D:]), mean_weight)
+        )
+        return lax.rsqrt(var * (HEADS / D) + NORM_EPS)
+
+    def normalise(layer, index, centred):
+        scale = head_scale(centred)
+        normal = centred * scale
+        if layer:
+            where = block(index)
+            x_keep[where, :] = normal
+            r_keep[where, :] = scale
+        high, low = halves(normal)
+        s_acc[layer, index // steps] += dot(
+            beside(high[:, :D], low[:, :D]), beside(high[:, D:], low[:, D:]), 0, 0
+        )
+
+    def quarters(value):
+        half_row, half_col = value.shape[0] // 2, value.shape[1] // 2
+        return (
+            value[:half_row, :half_col]
+            + value[half_row:, :half_col]
+            + (value[:half_row, half_col:] + value[half_row:, half_col:])
+        )
+
+    def summarise(layer):
+        weight = attn_ref[layer]
+        key_gain = vector("key_gain", layer).reshape(1, D)
+        value_gain = vector("value_gain", layer).reshape(1, D)
+        key_column = jnp.sum(eye * key_gain, 1, keepdims=True)
+        for s in range(count):
+            plain = jnp.where(blocks, quarters(s_acc[layer, s]), 0.0) * (1.0 / points)
+            summary = key_column * plain * value_gain
+            mixed = exact(summary, weight[:, 3 * D :])
+            both = exact(weight[:, :D], mixed)
+            n_keep[layer, s] = both
+            small_keep[layer, s, 0] = plain
+            small_keep[layer, s, 1] = summary
+            small_keep[layer, s, 2] = mixed
+            if layer == 0:
+                rows = exact(lift_rows, eye + both)
+                mid_rows[s] = rows
+                w0_g[s] = lift_weight(rows)
+                w0_u[s] = lift_weight(exact(rows, ffn_ref[0, 0]))
+            else:
+                pair, rest = tall6_weight(both)
+                wz[s, : 2 * D, :] = pair
+                wz[s, 2 * D :, :D] = rest
+                nt_keep[s] = tall4_weight(both.T)
+
+    def feed(layer, index, mid, inner):
+        where = block(index)
+        act, slope = gelu_pair(inner + vector("inner_bias", layer))
+        slope_keep[layer, where, :] = slope
+        pieces = thirds(act)
+        act_keep[layer, where, :] = beside(pieces[0], pieces[1])
+        return mid + tall6(pieces, (w_out0[layer], w_out1[layer])) + vector("outer_bias", layer)
+
+    def front_zero(index, _):
+        normalise(0, index, dot(lifted[block(index), :], w0_kv[...]))
+        return 0
+
+    lax.fori_loop(0, rows_all, front_zero, 0)
+    summarise(0)
+
+    def layer_zero(index, _):
+        where = block(index)
+        s = index // steps
+        data = lifted[where, :]
+        out = feed(0, index, dot(data, w0_g[s]), dot(data, w0_u[s]))
+        d_keep[where, :] = out
+        pieces = thirds(out)
+        h1_keep[where, :] = beside(*pieces)
+        normalise(1, index, wide6(pieces, w_kv[...]))
+        return 0
+
+    lax.fori_loop(0, rows_all, layer_zero, 0)
+    summarise(1)
+
+    def pieces_of(ref, where, number=3):
+        value = ref[where, : number * D]
+        return [value[:, i * D : (i + 1) * D] for i in range(number)]
+
+    def layer_one(index, _):
+        where = block(index)
+        s = index // steps
+        pieces = pieces_of(h1_keep, where)
+        mid = d_keep[where, :] + tall6(pieces, (wz[s, : 2 * D, :], wz[s, 2 * D :, :D]))
+        pieces = thirds(mid)
+        mid_keep[where, :] = beside(pieces[0], pieces[1])
+        out = feed(1, index, mid, wide6(pieces, w_in[...]))
+        h2_keep[where, :] = beside(*thirds(out))
+        return 0
+
+    lax.fori_loop(0, rows_all, layer_one, 0)
+
+    def dense_rows(part):
+        start = D + (part - 1) * FREQ if part else 0
+        return dense_ref[start : start + (FREQ if part else D), :]
+
+    proj0, proj1 = tall6_weight(doubled(dense_rows(0)))
+    locals6 = [tall6_weight(doubled(dense_rows(part))) for part in (1, 2, 3)]
+    locals4 = [tall4_weight(doubled(dense_rows(part).T)) for part in (1, 2, 3)]
+    own = lax.broadcasted_iota(jnp.int32, (2 * count * MODES, MODES * D), 1) // D == lax.rem(
+        lax.broadcasted_iota(jnp.int32, (2 * count * MODES, MODES * D), 0), MODES
+    )
+
+    def mode_rows(coef):
+        cosine, sine = coef[:MODES], coef[MODES:]
+        c = [cosine[:, s * FREQ : (s + 1) * FREQ] for s in range(count)]
+        d = [sine[:, s * FREQ : (s + 1) * FREQ] for s in range(count)]
+        return above(
+            *[beside(c[s], d[s]) for s in range(count)], *[beside(d[s], -c[s]) for s in range(count)]
+        )
+
+    def spread_rows(rows):
+        return jnp.where(own, beside(*([rows] * MODES)), 0.0)
+
+    def unpack(rows):
+        lead = count * MODES
+        return above(
+            *[beside(*[rows[j * lead + s * MODES : j * lead + (s + 1) * MODES] for s in range(count)]) for j in (0, 1)]
+        )
+
+    def pack(value):
+        return above(
+            *[
+                value[j * MODES : (j + 1) * MODES, s * FREQ : (s + 1) * FREQ]
+                for j in (0, 1)
+                for s in range(count)
+            ]
+        )
+
+    def set_stack(value):
+        high, middle, low = thirds(value)
+        stack_ref[...] = above(
+            high, high, middle, middle, low, high, jnp.zeros((4 * MODES, D), BF16)
+        )
+
+    def take_coef(index, high, low):
+        coef_acc[...] += dot(trow_ref[index], beside(high, low))
+
+    def mix_forward(layer):
+        coef = quarters(coef_acc[...]) * (1.0 / math.sqrt(points))
+        coef_acc[...] = jnp.zeros_like(coef_acc)
+        rows = mode_rows(coef)
+        coef_keep[layer] = rows
+        set_stack(unpack(exact(spread_rows(rows), spec_ref[layer])) * (1.0 / math.sqrt(MODES)))
+
+    def mix_back(layer):
+        cot = pack(quarters(coef_acc[...])) * (1.0 / math.sqrt(MODES))
+        coef_acc[...] = jnp.zeros_like(coef_acc)
+        g_spec[layer] = exact(spread_rows(coef_keep[layer]), cot, 0, 0)
+        wide = jnp.where(own, exact(cot, spec_ref[layer], 1, 1), 0.0)
+        kept = wide[:, :D]
+        for k in range(1, MODES):
+            kept = kept + wide[:, k * D : (k + 1) * D]
+        lead = count * MODES
+        first, second = kept[:lead], kept[lead:]
+        rows = above(first[:, :FREQ] - second[:, FREQ:], first[:, FREQ:] + second[:, :FREQ])
+        set_stack(unpack(rows) * (1.0 / math.sqrt(points)))
+
+    def project_step(index, _):
+        where = block(index)
+        first = h2_keep[block(index), :]
+        second = h2_keep[block(index + steps), :]
+        pieces = [beside(first[:, i * D : (i + 1) * D], second[:, i * D : (i + 1) * D]) for i in range(3)]
+        field = tall6(pieces, (proj0, proj1)) + vector("proj_bias", 0)
+        pieces = thirds(field)
+        z_keep[0, where, :] = beside(*pieces)
+        take_coef(index, pieces[0], pieces[1])
+        return 0
+
+    lax.fori_loop(0, steps, project_step, 0)
+    mix_forward(0)
+
+    def fourier_field(layer, where):
+        pieces = pieces_of(z_keep.at[layer], where)
+        inner = dot(table_ref[where, :], stack_ref[...]) + (
+            tall6(pieces, locals6[layer]) + vector("fourier_bias", layer)
+        )
+        return gelu_pair(inner)
+
+    def fourier_one(index, _):
+        where = block(index)
+        field, slope = fourier_field(0, where)
+        zs_keep[where, :] = slope
+        pieces = thirds(field)
+        z_keep[1, where, :] = beside(*pieces)
+        take_coef(index, pieces[0], pieces[1])
+        return 0
+
+    lax.fori_loop(0, steps, fourier_one, 0)
+    mix_forward(1)
+
+    lane = lax.broadcasted_iota(jnp.int32, (2 * D, 2 * D), 1)
+    row = lax.broadcasted_iota(jnp.int32, (2 * D, 2 * D), 0)
+    inner_row = lax.rem(row, D)
+    same = row // D == lax.rem(lane, D) // FREQ
+    pick_target = (lane < D) & (inner_row >= 15) & (inner_row < 18)
+    pick_mask = (lane >= D) & (inner_row == 18)
+    spread = jnp.where(same & (pick_target | pick_mask), 1.0, 0.0).astype(BF16)
+    out_row = vector("head_out", 0)
+    out_column = jnp.sum(eye * out_row, 1, keepdims=True)
+    half_blocks = (
+        lax.broadcasted_iota(jnp.int32, (D, D), 0) // FREQ == lax.broadcasted_iota(jnp.int32, (D, D), 1) // FREQ
+    )
+    out_weight = tall6_weight(jnp.where(half_blocks, out_column, 0.0))
+
+    def pair_product(first, second):
+        return dot(beside(*first), beside(*second), 0, 0)
+
+    def loss_step(index, _):
+        where = block(index)
+        field, slope = fourier_field(1, where)
+        pieces = thirds(field)
+        hidden, hidden_slope = gelu_pair(tall6(pieces, locals6[2]) + vector("head_bias", 0))
+        pred = tall6(thirds(hidden), out_weight)
+        known = dot(beside(lifted[where, :], lifted[block(index + steps), :]), spread)
+        diff = pred - known[:, :D]
+        valid = known[:, D:]
+        cot = (2.0 * valid) * diff
+        b_acc[0:8, :D] += column_sum(valid * diff * diff)
+        b_acc[8:16, :D] += column_sum(valid)
+        b_acc[16:24, :D] += column_sum(hidden * cot)
+        cot = cot * out_row * hidden_slope
+        b_acc[24:32, :D] += column_sum(cot)
+        split = halves(cot)
+        sq_acc[2] += pair_product(pieces[:2], split)
+        cot = tall4(split, locals4[2]) * slope
+        b_acc[32:40, :D] += column_sum(cot)
+        split = halves(cot)
+        e_keep[where, :] = beside(*split)
+        sq_acc[1] += pair_product(pieces_of(z_keep.at[1], where, 2), split)
+        take_coef(index, *split)
+        return 0
+
+    lax.fori_loop(0, steps, loss_step, 0)
+    mix_back(1)
+
+    def fourier_cot(layer, where):
+        return tall4(pieces_of(e_keep, where, 2), locals4[layer]) + dot(table_ref[where, :], stack_ref[...])
+
+    def fourier_back(index, _):
+        where = block(index)
+        cot = fourier_cot(1, where) * zs_keep[where, :]
+        b_acc[40:48, :D] += column_sum(cot)
+        split = halves(cot)
+        e_keep[where, :] = beside(*split)
+        sq_acc[0] += pair_product(pieces_of(z_keep.at[0], where, 2), split)
+        take_coef(index, *split)
+        return 0
+
+    lax.fori_loop(0, steps, fourier_back, 0)
+    mix_back(0)
+    turned = dense_rows(0).T
+    proj_back = wide4_weight(doubled(turned))
+
+    def project_back(index, _):
+        where = block(index)
+        later = block(index + steps)
+        cot = fourier_cot(0, where)
+        b_acc[48:56, :D] += column_sum(cot)
+        split = halves(cot)
+        first = pieces_of(h2_keep, where, 2)
+        second = pieces_of(h2_keep, later, 2)
+        p_acc[...] += dot(beside(first[0], second[0], first[1], second[1]), beside(*split), 0, 0)
+        rows = wide4(split, proj_back)
+        d_keep[where, :] = rows[:, :D]
+        d_keep[later, :] = rows[:, D:]
+        return 0
+
+    lax.fori_loop(0, steps, project_back, 0)
+
+    def feed_back(layer, index, cot):
+        where = block(index)
+        base = 56 + layer * 16
+        b_acc[base : base + 8, :D] += column_sum(cot)
+        split = halves(cot)
+        act = act_keep[layer, where, :]
+        w2_acc[layer] += dot(beside(*split), act[:, :FF], 0, 0)
+        w2_acc[layer, :D, :] += dot(split[0], act[:, FF:], 0, 0)
+        inner = wide4(split, w_outt[layer]) * slope_keep[layer, where, :]
+        b_acc[base + 8 : base + 16, :] += column_sum(inner)
+        return split, halves(inner)
+
+    def layer_one_back(index, _):
+        where = block(index)
+        cot = d_keep[where, :]
+        _, (high, low) = feed_back(1, index, cot)
+        mid = mid_keep[where, :]
+        w1_acc[...] += dot(mid, high, 0, 0)
+        w1_acc[:D, :] += dot(mid[:, :D], low, 0, 0)
+        cot = cot + tall4((high, low), w_int[...])
+        d_keep[where, :] = cot
+        y_acc[index // steps] += pair_product(pieces_of(h1_keep, where, 2), halves(cot))
+        return 0
+
+    lax.fori_loop(0, rows_all, layer_one_back, 0)
+
+    def attend_back(layer, products):
+        weight = attn_ref[layer]
+        query, outer = weight[:, :D], weight[:, 3 * D :]
+        key_gain, value_gain = vector("key_gain", layer), vector("value_gain", layer)
+        key_column = jnp.sum(eye * key_gain, 1, keepdims=True)
+        key_total = jnp.zeros((D, 1), F32)
+        value_total = jnp.zeros((1, D), F32)
+        query_grad = jnp.zeros((D, D), F32)
+        outer_grad = jnp.zeros((D, D), F32)
+        for s in range(count):
+            plain, summary, mixed = small_keep[layer, s, 0], small_keep[layer, s, 1], small_keep[layer, s, 2]
+            turned = exact(query, products[s], 0, 0)
+            outer_grad += exact(summary, turned, 0, 0)
+            query_grad += exact(products[s], mixed, 1, 1)
+            cot = jnp.where(blocks, exact(turned, outer, 1, 1), 0.0)
+            both = cot * plain
+            key_total += jnp.sum(both * value_gain, 1, keepdims=True)
+            value_total += jnp.sum(both * key_column, 0, keepdims=True)
+            scaled = key_column * cot * value_gain * (1.0 / points)
+            t_keep[s, 0] = tall4_weight(scaled.T)
+            t_keep[s, 1] = tall4_weight(scaled)
+        g_attn[layer, :, :D] = query_grad
+        g_attn[layer, :, 3 * D :] = outer_grad
+        return jnp.sum(eye * key_total, 0, keepdims=True), value_total
+
+    gains = [None, None]
+    gains[1] = attend_back(1, [quarters(y_acc[s]) for s in range(count)])
+
+    def norm_back(index, normal, scale):
+        s = index // steps
+        key, value = normal[:, :D], normal[:, D:]
+        key_cot = tall4(halves(value), t_keep[s, 0])
+        value_cot = tall4(halves(key), t_keep[s, 1])
+        mean = dot(beside(*halves(key_cot * key)), mean_weight) * (HEADS / D)
+        return beside(scale[:, :D] * (key_cot - key * mean), scale[:, D:] * (value_cot - value * mean))
+
+    def middle_back(index, _):
+        where = block(index)
+        s = index // steps
+        cot = norm_back(index, x_keep[where, :], r_keep[where, :])
+        high, low = halves(cot)
+        kept = h1_keep[where, : 2 * D]
+        kv_acc[...] += dot(kept, high, 0, 0)
+        kv_acc[:D, :] += dot(kept[:, :D], low, 0, 0)
+        out = d_keep[where, :]
+        out = out + tall4(halves(out), nt_keep[s]) + tall4((high, low), w_kvt[...])
+        outer, inner = feed_back(0, index, out)
+        v_acc[s] += dot(lrows[index], beside(*outer))
+        u_acc[s] += dot(lrows[index], beside(*inner))
+        return 0
+
+    lax.fori_loop(0, rows_all, middle_back, 0)
+
+    def lift_sum(value):
+        value = fold(value)
+        return above(
+            value[0:1] + value[1:2] + value[2:3],
+            value[3:4] + value[4:5] + value[5:6],
+            value[6:7],
+            jnp.zeros((5, value.shape[1]), F32),
+        )
+
+    inner_rows = [lift_sum(u_acc[s]) for s in range(count)]
+    value_rows = [lift_sum(v_acc[s]) + exact(inner_rows[s], ffn_ref[0, 0], 1, 1) for s in range(count)]
+    gains[0] = attend_back(0, [exact(lift_rows, value_rows[s], 0, 0) for s in range(count)])
+
+    def front_back(index, _):
+        centred = dot(lifted[block(index), :], w0_kv[...])
+        scale = head_scale(centred)
+        cot = norm_back(index, centred * scale, scale)
+        vt_acc[...] += dot(lrows[index], beside(*halves(cot)))
+        return 0
+
+    lax.fori_loop(0, rows_all, front_back, 0)
+
+    turned = lift_sum(vt_acc[...])
+    lift_grad = exact(turned, cent_keep[0], 1, 1)
+    for s in range(count):
+        lift_grad += value_rows[s] + exact(value_rows[s], n_keep[0, s], 1, 1)
+    joined = [exact(lift_rows, turned, 0, 0), kv_acc[:D, :] + kv_acc[D:, :]]
+    for layer in range(LAYERS):
+        g_attn[layer, :, D : 2 * D] = exact(joined[layer][:, :D], centre)
+        g_attn[layer, :, 2 * D : 3 * D] = exact(joined[layer][:, D:], centre)
+        g_ffn[layer, 1] = w2_acc[layer, :D, :] + w2_acc[layer, D:, :]
+
+    first = exact(mid_rows[0], inner_rows[0], 0, 0)
+    for s in range(1, count):
+        first += exact(mid_rows[s], inner_rows[s], 0, 0)
+    g_ffn[0, 0] = first
+    g_ffn[1, 0] = w1_acc[:D, :] + w1_acc[D:, :]
+    sums = p_acc[...]
+    sums = fold(sums[: 2 * D] + sums[2 * D :])
+    g_dense[:D, :] = sums[:D, :FREQ] + sums[D:, FREQ:]
+    for part in range(3):
+        sums = quarters(sq_acc[part])
+        start = D + part * FREQ
+        g_dense[start : start + FREQ, :] = sums[:FREQ, :FREQ] + sums[FREQ:, FREQ:]
+
+    def bias(slot, width=D):
+        return jnp.sum(b_acc[slot * 8 : slot * 8 + 8, :width], 0, keepdims=True)
+
+    rows = [lift_grad[0:1], lift_grad[1:2], lift_grad[2:3]]
+    for layer in range(LAYERS):
+        inner = bias(8 + 2 * layer, FF)
+        rows += [gains[layer][0], gains[layer][1], inner[:, :D], inner[:, D:], bias(7 + 2 * layer)]
+    short = [fold(bias(slot)) for slot in (6, 5, 4, 3, 2)]
+    rows += [beside(short[0], short[1]), beside(short[2], short[3]), beside(short[4], jnp.zeros((1, FREQ), F32))]
+    g_vec[...] = above(*rows)
+    lanes = lax.broadcasted_iota(jnp.int32, (1, D), 1)
+    first = jnp.where(lax.rem(lanes, FREQ) == 0, bias(0), 0.0)
+    second = jnp.where(lax.rem(lanes, FREQ) == 0, bias(1), 0.0)
+    g_loss[...] = above(first, second, jnp.zeros((6, D), F32))
+
+
+def tables(points):
+    order = np.arange(MODES)[:, None]
+    angle = (order * np.arange(points)[None, :]) % points * (2.0 * math.pi / points)
+    full = np.concatenate([np.cos(angle), np.sin(angle)], 0).astype(np.float32)
+    kind = np.dtype(ml_dtypes.bfloat16)
+    high = full.astype(kind)
+    rest = full - high.astype(np.float32)
+    middle = rest.astype(kind)
+    low = (rest - middle.astype(np.float32)).astype(kind)
+    zero = np.zeros((4 * MODES, points), kind)
+    column = np.concatenate([high, middle, high, middle, high, low, zero], 0).T
+    row = np.concatenate([high, middle], 0).reshape(4 * MODES, points // ROWS, ROWS).transpose(1, 0, 2)
+    return np.ascontiguousarray(column), np.ascontiguousarray(row)
+
+
+def local_grads(inputs, attn_w, ffn_w, spec_w, dense_w, vec):
+    count, _, points = inputs.shape
+    total = count * points
+    steps = points // ROWS
+    column, row = tables(points)
+    vmem = pl.BlockSpec(memory_space=pltpu.VMEM)
+    scratch = [
+        ((total, D), BF16),
+        ((total // ROWS, 16, ROWS), BF16),
+        ((6 * D, 2 * D), BF16),
+        ((4 * D, 2 * D), BF16),
+        ((6 * D, FF), BF16),
+        ((2 * FF, 2 * D), BF16),
+        ((count, D, FF), BF16),
+        ((count, 8, D), F32),
+        ((LAYERS, 2 * FF, 2 * D), BF16),
+        ((LAYERS, 2 * FF, D), BF16),
+        ((LAYERS, 4 * D, FF), BF16),
+        ((total, 2 * D), F32),
+        ((total, 2 * D), F32),
+        ((LAYERS, total, FF), F32),
+        ((LAYERS, total, 2 * FF), BF16),
+        ((total, 2 * D), BF16),
+        ((total, 3 * D), BF16),
+        ((total, 3 * D), BF16),
+        ((FLAYERS, points, 3 * D), BF16),
+        ((points, D), F32),
+        ((points, 2 * D), BF16),
+        ((LAYERS, count, 2 * D, 2 * D), F32),
+        ((D, 2 * D), BF16),
+        ((count, D, D), BF16),
+        ((LAYERS, count, D, D), F32),
+        ((LAYERS, count, 3, D, D), F32),
+        ((count, 2 * D, 2 * D), BF16),
+        ((LAYERS, D, 2 * D), F32),
+        ((4 * MODES, 2 * D), F32),
+        ((FLAYERS, 2 * count * MODES, D), F32),
+        ((2 * D, D), BF16),
+        ((3, 2 * D, 2 * D), F32),
+        ((4 * D, 2 * D), F32),
+        ((count, 2 * D, 2 * D), F32),
+        ((LAYERS, 2 * D, FF), F32),
+        ((2 * D, FF), F32),
+        ((2 * D, 2 * D), F32),
+        ((count, 16, 2 * D), F32),
+        ((count, 16, 2 * FF), F32),
+        ((16, 4 * D), F32),
+        ((96, FF), F32),
+        ((total, D), F32),
+        ((count, 2, 2 * D, 2 * D), BF16),
+        ((count, 4 * D, 2 * D), BF16),
+    ]
+    shapes = [attn_w.shape, ffn_w.shape, spec_w.shape, dense_w.shape, vec.shape, (8, D)]
+    return pl.pallas_call(
+        local_kernel,
+        out_shape=[jax.ShapeDtypeStruct(shape, F32) for shape in shapes],
+        in_specs=[vmem] * 8,
+        out_specs=[vmem] * 6,
+        scratch_shapes=[pltpu.VMEM(*item) for item in scratch],
+        compiler_params=pltpu.CompilerParams(vmem_limit_bytes=64 * 2**20 - 2**17),
+    )(inputs, attn_w, ffn_w, spec_w, dense_w, vec, jnp.asarray(column), jnp.asarray(row))
+
+
+def fast_body(samples_in, target, mask, attn_w, ffn_w, spec_w, dense_w, vectors, *moments):
+    packed = jnp.concatenate([samples_in, target[:, None], mask.astype(F32)[:, None]], 1)
+    whole = lax.all_to_all(packed, "pts", split_axis=0, concat_axis=2, tiled=True)
+    vec = jnp.pad(vectors, (0, -vectors.shape[0] % D)).reshape(-1, D)
+    pieces = local_grads(
+        whole, attn_w, ffn_w, spec_w.reshape(FLAYERS, MODES * 2 * FREQ, FREQ), dense_w, vec
+    )
+    summed = lax.psum(tuple(pieces), ("dp", "pts"))
+    loss_sum, valid_count = jnp.sum(summed[5][0]), jnp.sum(summed[5][1])
+    grads = (
+        summed[0],
+        summed[1],
+        summed[2].reshape(spec_w.shape),
+        summed[3],
+        summed[4].reshape(-1)[: vectors.shape[0]],
+    )
+    grads = tuple(grad * (1.0 / valid_count) for grad in grads)
+    params = (attn_w, ffn_w, spec_w, dense_w, vectors)
+    return tuple(finish(loss_sum, valid_count, params, grads, moments[:5], moments[5:]))
+
+
+def choose_body(*arrays):
+    samples_in = arrays[0]
+    parts = lax.axis_size("pts")
+    regular = samples_in.shape[0] == 2 * parts and samples_in.shape[2] * parts % ROWS == 0
+    return (fast_body if regular else body)(*arrays)
+
+
 def solution(mesh):
     placed = (
         P("dp", None, "pts"),
@@ -369,7 +1159,7 @@
         P(),
     )
     return jax.shard_map(
-        body,
+        choose_body,
         mesh=mesh,
         in_specs=placed,
         out_specs=(

time: 1410 us -> 285 us (0.20)
  waiting for transfers between devices: 531 us -> 96.4 us
  matrix products: 249 us -> 0 us
  blocking collectives: 276 us -> 38.9 us
  local copies, waits for them, and re-layouts: 228 us -> 10.3 us
  Pallas kernels: 0 us -> 91.2 us
  other arithmetic: 84 us -> 21.7 us
    psum x5 -> x1, waiting for transfers between devices: 375 us -> 92.5 us  [fast_body(): summed = lax.psum(tuple(pieces), ('dp', 'pts'))]
    dot_general x82 -> x0, matrix products: 249 us -> none  [the longest x6 43 us: ffn_block(): jnp.einsum('...f,df->...d', jax.nn.gelu(inner), weight[1], precision=HIGH)]
    all_to_all x5 -> x0, blocking collectives: 133 us -> none  [the longest x2 58.2 us: fourier_back(): lax.all_to_all(grad_back, 'pts', split_axis=2, concat_axis=1, tiled=True)]
    reduce_scatter x2 -> x0, waiting for transfers between devices: 116 us -> none  [fourier_back(): lax.psum_scatter(grad_full, 'pts', scatter_dimension=2, tiled=True)]
    pallas_call x0 -> x1, Pallas kernels: none -> 91.2 us  [local_grads(): pl.pallas_call(local_kernel, out_shape=[jax.ShapeDtypeStruct(shape, F32)...]
    unnamed x286 -> x59, local copies, waits for them, and re-layouts: 71.2 us -> 5.78 us
    all_gather x2 -> x0, blocking collectives: 63.2 us -> none  [fourier_mix(): full = lax.all_gather(own_coef, 'pts', axis=2, tiled=True)]
    psum x2 -> x1, blocking collectives: 79.6 us -> 38.9 us  [fast_body(): summed = lax.psum(tuple(pieces), ('dp', 'pts'))]
  transfers between devices with their start and end apart: 10 -> 2, of which waited for: 9 -> 2; matrix products, arithmetic and copies ran while one was open for 6% -> 2% of each run, Pallas kernels for 0% -> 0%
where the time goes in v1:
time: 285 us; the launch traced here: 284 us
  waiting for transfers between devices  96.4 us (34%)
  Pallas kernels  91.2 us (32%)
  blocking collectives  38.9 us (14%)
  other arithmetic  21.7 us (8%)
  between operations  18 us (6%)
  local copies, waits for them, and re-layouts  10.3 us (4%)
  starting transfers between devices  7.32 us (3%)
    psum x1, waiting for transfers between devices, fast_body(): summed = lax.psum(tuple(pieces), ('dp', 'pts'))  92.5 us
    pallas_call x1, Pallas kernels, local_grads(): pl.pallas_call(local_kernel, out_shape=[jax.ShapeDtypeStruct(shape, F32)...  91.2 us
    psum x1, blocking collectives, fast_body(): summed = lax.psum(tuple(pieces), ('dp', 'pts'))  38.9 us
    all_to_all x1, starting transfers between devices, fast_body(): lax.all_to_all(packed, 'pts', split_axis=0, concat_axis=2, tiled=True)  7.28 us
    reduce_sum x4, other arithmetic, trust_step(): weight_norm = jnp.sqrt(jnp.sum(weight * weight, axes))  7.08 us
    convert_element_type x5, other arithmetic, finish(): fresh.astype(jnp.bfloat16)  6.33 us
    unnamed x59, local copies, waits for them, and re-layouts  5.78 us
  transfers between devices with their start and end apart: 2, of which 2 were waited for; matrix products, arithmetic and copies ran while one was open for 2% of the time, Pallas kernels for 0%

profile of v1, /device:TPU:0, one launch (start us, length us, event | category | flops | bytes accessed | tf_op | source)
XLA Modules:
  0.0 283.8 jit_solution(330842034485018386)
XLA Ops:
  7.2 0.7 copy.57
  7.9 0.7 convert_bitcast_fusion
  8.7 1.4 pad_maximum_fusion
  10.1 7.3 %all-to-all-start = ((f32[16,4,256]{2,1,0:T(4,128)}), f32[16,4,256]{2,1,0:T(4,128)S(1)}, u32[]{:S(2)}, u32[]{:S(2)}) async-start(f32[16,4,256]{2,1,0:T(4,128)} %pad_maximum_fusion), calls=%async_computation | async-start | bytes 131072 | tf_op jit(solution)/shard_map/all_to_all | solution.py:1114
  17.5 1.7 copy.60.dense_ref
  19.1 1.3 pad_bitcast_fusion.vec_ref
  20.4 3.9 %all-to-all-done = f32[16,4,256]{2,1,0:T(4,128)S(1)} async-done(((f32[16,4,256]{2,1,0:T(4,128)}), f32[16,4,256]{2,1,0:T(4,128)S(1)}, u32[]{:S(2)}, u32[]{:S(2)}) %all-to-all-start) | async-done | bytes 65568 | tf_op jit(solution)/shard_map/all_to_all | solution.py:1114
  24.3 0.7 all_to_all.16.inputs_ref
  25.0 91.2 %shard_map.387 = (f32[2,128,512]{2,1,0:T(8,128)}, f32[2,2,128,256]{3,2,1,0:T(8,128)}, f32[2,2048,64]{2,1,0:T(8,128)}, f32[320,64]{1,0:T(8,128)}, f32[16,128]{1,0:T(8,128)}, /*index=5*/f32[8,128]{1,0:T(8,128)}) custom-call(f32[2,4,2048]{2,1,0:T(4,128)} %all_to_all.16.inputs_ref, f32[2,128,512]{2,1,0:T(8,128)} %attn_ref.1, f32[2,2,128,256]{3,2,1,0:T(8,128)} %ffn_ref.1, ...), custom_call_target="tpu_custom_call" | custom-call | tf_op jit(solution)/shard_map/pallas_call | solution.py:1102
  116.3 0.8 copy-done.16
  117.1 0.6 multiply_reduce_fusion.7
  118.7 38.9 %all-reduce.1 = (f32[8,128]{1,0:T(8,128)S(1)}, f32[2048]{0:T(1024)S(1)}) all-reduce(f32[8,128]{1,0:T(8,128)S(1)} %copy-done.25, f32[2048]{0:T(1024)S(1)} %bitcast.26), channel_id=1, replica_groups=mesh['dp'=4,'pts'=8] {'dp','pts'}, use_global_device_ids=true, to_apply=%region_0.1 | all-reduce | flops 3072 | bytes 24576 | tf_op jit(solution)/shard_map/psum | solution.py:1119
  157.6 0.6 slice_reduce_fusion
  158.9 0.6 multiply_reduce_fusion.8
  161.0 0.6 fusion.5
  161.6 92.5 %all-reduce.5.cloned.1.call-done = (f32[2,128,512]{2,1,0:T(8,128)}, f32[2,2,128,256]{3,2,1,0:T(8,128)}, f32[2,2048,64]{2,1,0:T(8,128)}, f32[320,64]{1,0:T(8,128)}) async-done(((f32[2,128,512]{2,1,0:T(8,128)}, f32[2,2,128,256]{3,2,1,0:T(8,128)}, f32[2,2048,64]{2,1,0:T(8,128)}, f32[320,64]{1,0:T(8,128)}), (f32[2,128,512]{2,1,0:T(8,128)}, f32[2,2,128,256]{3,2,1,0:T(8,128)}, f32[2,2048,64]{2,1,0:T(8,128)}, ...) | async-done | bytes 2179088 | tf_op jit(solution)/shard_map/psum | solution.py:1119
  254.2 1.7 multiply_reduce_fusion.6
  256.6 3.2 %broadcast_multiply_fusion = f32[2,2048,64]{2,1,0:T(8,128)} fusion(f32[2,2048,64]{2,1,0:T(8,128)} %get-tuple-element.101, f32[]{:T(128)S(6)} %div.79), kind=kLoop, calls=%fused_computation.7 | loop fusion | flops 262144 | bytes 2097156 | tf_op jit(solution)/shard_map/mul | solution.py:1128
  259.7 0.8 copy.68
  260.5 0.8 copy.69
  261.3 0.1 fusion.7
  261.4 0.7 copy.71
  262.2 0.8 copy.70
  262.9 1.7 multiply_reduce_fusion.5
  264.7 2.1 multiply_reduce_fusion.3
  266.9 1.2 fusion.13
  268.1 2.6 multiply_reduce_fusion.1
  270.8 1.5 fusion.11
  272.3 2.9 %fusion.9 = (bf16[2,16,2,64,64]{4,3,2,1,0:T(8,128)(2,1)}, f32[2,16,2,64,64]{4,3,2,1,0:T(8,128)}) fusion(f32[2,16,2,64,64]{4,3,2,1,0:T(8,128)S(1)} %copy-done, f32[2,16,2,64,64]{4,3,2,1,0:T(8,128)S(1)} %get-tuple-element.116, f32[2,16,2,64,64]{4,3,2,1,0:T(8,128)S(1)} %get-tuple-element.117, f32[2]{0:T(128)S(1)} %get-tuple-element.114), kind=kLoop, calls=%fused_computation.51 | loop fusion | flops 2359296 | bytes 4718600 | tf_op jit(solution)/shard_map/convert_element_type | solution.py:250
  275.2 0.6 concatenate.15
  275.8 0.6 concatenate.13
  276.4 0.6 concatenate.14
  (59 shorter events, 0.5 us)
Async XLA Ops:
  10.1 14.2 %all-to-all-start = ((f32[16,4,256]{2,1,0:T(4,128)}), f32[16,4,256]{2,1,0:T(4,128)S(1)}, u32[]{:S(2)}, u32[]{:S(2)}) async-start(f32[16,4,256]{2,1,0:T(4,128)} %pad_maximum_fusion), calls=%async_computation | async-start | bytes 131072 | tf_op jit(solution)/shard_map/all_to_all | solution.py:1114
  17.4 236.8 %all-reduce.5.cloned.1.call-start = ((), (), s32[]{:S(2)}) async-start(), calls=%async_computation.1 | async-start | bytes 6619136 | tf_op jit(solution)/shard_map/psum | solution.py:1119
  116.2 0.9 copy-start.16
  116.2 2.2 copy-start.17
  116.2 2.3 copy-start.18
  116.2 2.4 copy-start.24
  116.2 2.4 copy-start.25
  116.3 42.7 %copy-start.19 = (f32[1984]{0:T(1024)S(1)}, f32[1984]{0:T(1024)}, u32[]{:S(2)}) copy-start(f32[1984]{0:T(1024)} %param.27) | copy-start | bytes 23812
  116.3 42.7 %copy-start.22 = (f32[1984]{0:T(1024)S(1)}, f32[1984]{0:T(1024)}, u32[]{:S(2)}) copy-start(f32[1984]{0:T(1024)} %param.37) | copy-start | bytes 23812
  116.3 42.7 %copy-start.23 = (f32[1984]{0:T(1024)S(1)}, f32[1984]{0:T(1024)}, u32[]{:S(2)}) copy-start(f32[1984]{0:T(1024)} %param.32) | copy-start | bytes 23812
  116.3 137.9 %copy-start.6 = (f32[320,64]{1,0:T(8,128)S(1)}, f32[320,64]{1,0:T(8,128)}, u32[]{:S(2)}) copy-start(f32[320,64]{1,0:T(8,128)} %copy.60.dense_ref) | copy-start | bytes 245764
  159.6 100.2 %copy-start.20 = (f32[1984]{0:T(1024)}, f32[1984]{0:T(1024)S(1)}, u32[]{:S(2)}) copy-start(f32[1984]{0:T(1024)S(1)} %get-tuple-element.105) | copy-start | bytes 23812
  159.6 100.2 %copy-start.21 = (f32[1984]{0:T(1024)}, f32[1984]{0:T(1024)S(1)}, u32[]{:S(2)}) copy-start(f32[1984]{0:T(1024)S(1)} %get-tuple-element.106) | copy-start | bytes 23812
  256.5 6.4 %copy-start.4 = (f32[2,128,512]{2,1,0:T(8,128)S(1)}, f32[2,128,512]{2,1,0:T(8,128)}, u32[]{:S(2)}) copy-start(f32[2,128,512]{2,1,0:T(8,128)} %attn_ref.1) | copy-start | bytes 1572868
  256.5 6.4 %copy-start.13 = (f32[2,128,512]{2,1,0:T(8,128)S(1)}, f32[2,128,512]{2,1,0:T(8,128)}, u32[]{:S(2)}) copy-start(f32[2,128,512]{2,1,0:T(8,128)} %param.33) | copy-start | bytes 1572868
  256.6 6.4 %copy-start.14 = (f32[2,128,512]{2,1,0:T(8,128)S(1)}, f32[2,128,512]{2,1,0:T(8,128)}, u32[]{:S(2)}) copy-start(f32[2,128,512]{2,1,0:T(8,128)} %param.28) | copy-start | bytes 1572868
  261.3 3.4 %copy-start.5 = (f32[2,2,128,256]{3,2,1,0:T(8,128)S(1)}, f32[2,2,128,256]{3,2,1,0:T(8,128)}, u32[]{:S(2)}) copy-start(f32[2,2,128,256]{3,2,1,0:T(8,128)} %ffn_ref.1) | copy-start | bytes 1572868
  261.3 3.4 %copy-start.15 = (f32[2,2,128,256]{3,2,1,0:T(8,128)S(1)}, f32[2,2,128,256]{3,2,1,0:T(8,128)}, u32[]{:S(2)}) copy-start(f32[2,2,128,256]{3,2,1,0:T(8,128)} %param.34) | copy-start | bytes 1572868
  262.9 5.2 %copy-start.7 = (f32[2,16,2,64,64]{4,3,2,1,0:T(8,128)S(1)}, f32[2,16,2,64,64]{4,3,2,1,0:T(8,128)}, u32[]{:S(2)}) copy-start(f32[2,16,2,64,64]{4,3,2,1,0:T(8,128)} %param.35) | copy-start | bytes 3145732
  262.9 5.2 %copy-start.8 = (f32[2,16,2,64,64]{4,3,2,1,0:T(8,128)S(1)}, f32[2,16,2,64,64]{4,3,2,1,0:T(8,128)}, u32[]{:S(2)}) copy-start(f32[2,16,2,64,64]{4,3,2,1,0:T(8,128)} %param.30) | copy-start | bytes 3145732
  264.7 3.4 %copy-start.9 = (f32[2,128,512]{2,1,0:T(8,128)}, f32[2,128,512]{2,1,0:T(8,128)S(1)}, u32[]{:S(2)}) copy-start(f32[2,128,512]{2,1,0:T(8,128)S(1)} %get-tuple-element.128) | copy-start | bytes 1572868
  264.7 3.4 %copy-start.10 = (f32[2,128,512]{2,1,0:T(8,128)}, f32[2,128,512]{2,1,0:T(8,128)S(1)}, u32[]{:S(2)}) copy-start(f32[2,128,512]{2,1,0:T(8,128)S(1)} %get-tuple-element.129) | copy-start | bytes 1572868
  264.7 3.4 %copy-start = (f32[2,16,2,64,64]{4,3,2,1,0:T(8,128)S(1)}, f32[2,16,2,64,64]{4,3,2,1,0:T(8,128)}, u32[]{:S(2)}) copy-start(f32[2,16,2,64,64]{4,3,2,1,0:T(8,128)} %param.25) | copy-start | bytes 3145732
  264.7 3.4 %copy-start.3 = (f32[2,2048,64]{2,1,0:T(8,128)S(1)}, f32[2,2048,64]{2,1,0:T(8,128)}, u32[]{:S(2)}) copy-start(f32[2,2048,64]{2,1,0:T(8,128)} %broadcast_multiply_fusion) | copy-start | bytes 3145732
  266.9 3.9 %copy-start.11 = (f32[2,2,128,256]{3,2,1,0:T(8,128)}, f32[2,2,128,256]{3,2,1,0:T(8,128)S(1)}, u32[]{:S(2)}) copy-start(f32[2,2,128,256]{3,2,1,0:T(8,128)S(1)} %get-tuple-element.122) | copy-start | bytes 1572868
  266.9 3.9 %copy-start.12 = (f32[2,2,128,256]{3,2,1,0:T(8,128)}, f32[2,2,128,256]{3,2,1,0:T(8,128)S(1)}, u32[]{:S(2)}) copy-start(f32[2,2,128,256]{3,2,1,0:T(8,128)S(1)} %get-tuple-element.123) | copy-start | bytes 1572868
  270.7 4.5 %copy-start.1 = (f32[2,16,2,64,64]{4,3,2,1,0:T(8,128)}, f32[2,16,2,64,64]{4,3,2,1,0:T(8,128)S(1)}, u32[]{:S(2)}) copy-start(f32[2,16,2,64,64]{4,3,2,1,0:T(8,128)S(1)} %get-tuple-element.116) | copy-start | bytes 3145732
  270.7 4.4 %copy-start.2 = (f32[2,16,2,64,64]{4,3,2,1,0:T(8,128)}, f32[2,16,2,64,64]{4,3,2,1,0:T(8,128)S(1)}, u32[]{:S(2)}) copy-start(f32[2,16,2,64,64]{4,3,2,1,0:T(8,128)S(1)} %get-tuple-element.117) | copy-start | bytes 3145732
Sparse Core Ops, SparseCore 0:
  116.4 137.6 all-reduce.4

commit v2 on v1

--- a/solution.py
+++ b/solution.py
@@ -354,6 +354,7 @@
 F32 = jnp.float32
 BF16 = jnp.bfloat16
 ROWS = 512
+NVEC_ROWS = 16
 
 
 def dot(first, second, left=1, right=0, precision=None):
@@ -461,21 +462,170 @@
     return above(beside(weight, zero), beside(zero, weight))
 
 
-def local_kernel(
-    inputs_ref,
+MESH = pl.DeviceIdType.MESH
+
+
+def position():
+    dp, pts = lax.axis_index("dp"), lax.axis_index("pts")
+    x, core, z, y = dp // 2, dp % 2, pts // 2, pts % 2
+    return x, core, z, y
+
+
+def device_of(x, core, z, y):
+    return (2 * x + core, 2 * z + y)
+
+
+def device_at(number):
+    core, a, b, z = number // 16, number // 8 % 2, number // 4 % 2, number % 4
+    x = (1 - core) * a + core * b
+    y = (1 - core) * b + core * a
+    return device_of(x, core, z, y)
+
+
+class Route:
+    def __init__(self, rows, full, flat, landing, sends, receives, first):
+        x, core, z, y = position()
+        a = (1 - core) * x + core * y
+        b = (1 - core) * y + core * x
+        self.keep = (core, a, b, z)
+        self.rows, self.full, self.flat, self.landing = rows, full, flat, landing
+        self.sends, self.receives, self.first = sends, receives, first
+        self.peers = [
+            device_of(x, 1 - core, z, y),
+            device_of(x + (1 - core) * (1 - 2 * x), core, z, y + core * (1 - 2 * y)),
+            device_of(x + core * (1 - 2 * x), core, z, y + (1 - core) * (1 - 2 * y)),
+        ]
+        self.far = [device_of(x, core, (z + k) % 4, y) for k in (1, 2, 3)]
+        half, quarter, eighth, least = rows // 2, rows // 4, rows // 8, rows // 32
+        self.least = least
+        self.sizes = [half, quarter, eighth]
+        self.starts = [core * half, core * half + a * quarter, core * half + a * quarter + b * eighth]
+        self.own = self.starts[2] + z * least
+        self.others = [
+            (1 - core) * half,
+            core * half + (1 - a) * quarter,
+            core * half + a * quarter + (1 - b) * eighth,
+        ]
+
+    def area(self, start, size):
+        return pl.ds(pl.multiple_of(start, self.least), size)
+
+    def link(self, source, target, slot, device):
+        return pltpu.make_async_remote_copy(
+            src_ref=source,
+            dst_ref=target,
+            send_sem=self.sends.at[self.first + slot],
+            recv_sem=self.receives.at[self.first + slot],
+            device_id=device,
+            device_id_type=MESH,
+        )
+
+    def copies(self, stage, receiving=False):
+        z = self.keep[3]
+        if stage < 3:
+            place = self.landing.at[pl.ds(self.rows - 2 * self.sizes[stage], self.sizes[stage])]
+            source = self.flat.at[self.area(self.others[stage], self.sizes[stage])]
+            return [self.link(source, place, stage, self.peers[stage])]
+        if stage == 3:
+            found = []
+            for k in (1, 2, 3):
+                start = self.starts[2] + (z + k) % 4 * self.least
+                place = self.landing.at[pl.ds(self.rows - self.sizes[2] + (k - 1) * self.least, self.least)]
+                found.append(self.link(self.flat.at[self.area(start, self.least)], place, 2 + k, self.far[k - 1]))
+            return found
+        if stage == 4:
+            piece = self.full.at[self.area(self.own, self.least)]
+            found = []
+            for k in (1, 2, 3):
+                start = self.starts[2] + (z + 4 - k) % 4 * self.least if receiving else self.own
+                found.append(self.link(piece, self.full.at[self.area(start, self.least)], 5 + k, self.far[k - 1]))
+            return found
+        level = 7 - stage
+        size = self.sizes[level]
+        piece = self.full.at[self.area(self.starts[level], size)]
+        target = self.full.at[self.area(self.others[level], size)] if receiving else piece
+        return [self.link(piece, target, 4 + stage, self.peers[level])]
+
+    def start(self, stage):
+        if stage == 4 and self.flat is not None:
+            self.full[self.area(self.own, self.least), :] = self.flat[self.area(self.own, self.least), :]
+        for copy in self.copies(stage):
+            copy.start()
+
+    def finish(self, stage):
+        for copy in self.copies(stage, True):
+            copy.wait()
+        if stage < 3:
+            mine = self.area(self.starts[stage], self.sizes[stage])
+            place = pl.ds(self.rows - 2 * self.sizes[stage], self.sizes[stage])
+            self.flat[mine, :] += self.landing[place, :]
+        if stage == 3:
+            mine = self.area(self.own, self.least)
+            total = self.flat[mine, :]
+            for k in range(3):
+                total = total + self.landing[pl.ds(self.rows - self.sizes[2] + k * self.least, self.least), :]
+            self.flat[mine, :] = total
+
+    def step(self, stage):
+        self.finish(stage)
+        self.start(stage + 1)
+
+
+def spread_to_all(devices, mine, source_of, target, sends, receives, start):
+    def one(i, _):
+        other = lax.rem(mine + 1 + i, devices)
+        sender = lax.rem(mine + devices - 1 - i, devices)
+        copy = pltpu.make_async_remote_copy(
+            src_ref=source_of(other),
+            dst_ref=target.at[mine if start else sender],
+            send_sem=sends.at[i],
+            recv_sem=receives.at[i],
+            device_id=device_at(other),
+            device_id_type=MESH,
+        )
+        if start:
+            copy.start()
+        else:
+            copy.wait()
+        return 0
+
+    lax.fori_loop(0, devices - 1, one, 0)
+
+
+def step_kernel(
+    samples_ref,
+    target_ref,
+    mask_ref,
     attn_ref,
     ffn_ref,
     spec_ref,
-    dense_ref,
-    vec_ref,
+    turned_ref,
+    vectors_ref,
     table_ref,
     trow_ref,
-    g_attn,
-    g_ffn,
-    g_spec,
-    g_dense,
-    g_vec,
-    g_loss,
+    early_out,
+    late_out,
+    mode_out,
+    tail_out,
+    outgoing,
+    incoming,
+    vec_ref,
+    early,
+    early_land,
+    late,
+    late_land,
+    mode_send,
+    mode_land,
+    tail_send,
+    tail_land,
+    route_send,
+    route_recv,
+    point_send,
+    point_recv,
+    mode_sends,
+    mode_recvs,
+    tail_sends,
+    tail_recvs,
     lifted,
     lrows,
     w_kv,
@@ -521,7 +671,52 @@
     t_keep,
     wz,
 ):
-    count, points = inputs_ref.shape[0], inputs_ref.shape[2]
+    parts = samples_ref.shape[0] // 2
+    count = 2
+    points = samples_ref.shape[2] * parts
+    devices = FLAYERS * MODES
+    x, core, z, y = position()
+    pts = 2 * z + y
+    mine = 16 * core + 8 * ((1 - core) * x + core * y) + 4 * ((1 - core) * y + core * x) + z
+    early_route = Route(early.shape[0], early_out, early, early_land, route_send, route_recv, 0)
+    late_route = Route(late.shape[0], late_out, late, late_land, route_send, route_recv, 12)
+    mode_route = Route(mode_out.shape[0], mode_out, None, None, route_send, route_recv, 24)
+
+    barrier = pltpu.get_barrier_semaphore()
+
+    def greet(i, _):
+        pl.semaphore_signal(
+            barrier, inc=1, device_id=device_at(lax.rem(mine + 1 + i, devices)), device_id_type=MESH
+        )
+        return 0
+
+    lax.fori_loop(0, devices - 1, greet, 0)
+    for p in range(parts):
+        outgoing[p, 0:2, :] = samples_ref[2 * p]
+        outgoing[p, 2:4, :] = samples_ref[2 * p + 1]
+        outgoing[p, 4:6, :] = target_ref[2 * p : 2 * p + 2, :]
+        outgoing[p, 6:8, :] = mask_ref[2 * p : 2 * p + 2, :].astype(F32)
+    incoming[pts] = outgoing[pts]
+    pl.semaphore_wait(barrier, devices - 1)
+
+    def point_copy(k, start):
+        other = lax.rem(pts + k, parts)
+        sender = lax.rem(pts + parts - k, parts)
+        return pltpu.make_async_remote_copy(
+            src_ref=outgoing.at[other],
+            dst_ref=incoming.at[pts if start else sender],
+            send_sem=point_send.at[k - 1],
+            recv_sem=point_recv.at[k - 1],
+            device_id=(2 * x + core, other),
+            device_id_type=MESH,
+        )
+
+    for k in range(1, parts):
+        point_copy(k, True).start()
+    for i in range(NVEC_ROWS - 1):
+        vec_ref[i : i + 1, :] = vectors_ref[i * D : (i + 1) * D].reshape(1, D)
+    last = vectors_ref.shape[0] - (NVEC_ROWS - 1) * D
+    vec_ref[NVEC_ROWS - 1 :, :last] = vectors_ref[(NVEC_ROWS - 1) * D :].reshape(1, last)
     total = count * points
     steps = points // ROWS
     rows_all = total // ROWS
@@ -555,20 +750,6 @@
 
     def block(index):
         return pl.ds(pl.multiple_of(index * ROWS, ROWS), ROWS)
-
-    for s in range(count):
-        data = inputs_ref[s]
-        value, coord, target, valid = data[0:1], data[1:2], data[2:3], data[3:4]
-        one = jnp.ones_like(value)
-        vh, vm, vl = [item.astype(F32) for item in thirds(value)]
-        ch, cm, cl = [item.astype(F32) for item in thirds(coord)]
-        th, tm, tl = [item.astype(F32) for item in thirds(target)]
-        zero = jnp.zeros((D - 19, points), F32)
-        stack = above(vh, vm, vh, vm, vh, vl, ch, cm, ch, cm, ch, cl, one, one, one, th, tm, tl, valid, zero)
-        lifted[s * points : (s + 1) * points, :] = stack.T.astype(BF16)
-        short = above(vh, vm, vl, ch, cm, cl, one, jnp.zeros((9, points), F32)).astype(BF16)
-        for i in range(steps):
-            lrows[s * steps + i] = short[:, i * ROWS : (i + 1) * ROWS]
 
     lift_rows = above(
         vector("lift_value", 0), vector("lift_coord", 0), vector("lift_bias", 0), jnp.zeros((5, D), F32)
@@ -614,6 +795,23 @@
     u_acc[...] = jnp.zeros_like(u_acc)
     vt_acc[...] = jnp.zeros_like(vt_acc)
     b_acc[...] = jnp.zeros_like(b_acc)
+
+    for k in range(1, parts):
+        point_copy(k, False).wait()
+    whole = beside(*[incoming[p] for p in range(parts)])
+    for s in range(count):
+        value, coord = whole[2 * s : 2 * s + 1], whole[2 * s + 1 : 2 * s + 2]
+        target, valid = whole[4 + s : 5 + s], whole[6 + s : 7 + s]
+        one = jnp.ones_like(value)
+        vh, vm, vl = [item.astype(F32) for item in thirds(value)]
+        ch, cm, cl = [item.astype(F32) for item in thirds(coord)]
+        th, tm, tl = [item.astype(F32) for item in thirds(target)]
+        zero = jnp.zeros((D - 19, points), F32)
+        stack = above(vh, vm, vh, vm, vh, vl, ch, cm, ch, cm, ch, cl, one, one, one, th, tm, tl, valid, zero)
+        lifted[s * points : (s + 1) * points, :] = stack.T.astype(BF16)
+        short = above(vh, vm, vl, ch, cm, cl, one, jnp.zeros((9, points), F32)).astype(BF16)
+        for i in range(steps):
+            lrows[s * steps + i] = short[:, i * ROWS : (i + 1) * ROWS]
 
     def head_scale(centred):
         high, low = halves(centred * centred)
@@ -715,7 +913,7 @@
 
     def dense_rows(part):
         start = D + (part - 1) * FREQ if part else 0
-        return dense_ref[start : start + (FREQ if part else D), :]
+        return turned_ref[:, start : start + (FREQ if part else D)].T
 
     proj0, proj1 = tall6_weight(doubled(dense_rows(0)))
     locals6 = [tall6_weight(doubled(dense_rows(part))) for part in (1, 2, 3)]
@@ -769,7 +967,12 @@
     def mix_back(layer):
         cot = pack(quarters(coef_acc[...])) * (1.0 / math.sqrt(MODES))
         coef_acc[...] = jnp.zeros_like(coef_acc)
-        g_spec[layer] = exact(spread_rows(coef_keep[layer]), cot, 0, 0)
+        kept_rows = coef_keep[layer]
+        padded = beside(cot, jnp.zeros_like(cot))
+        for k in range(MODES):
+            for r in range(2 * count):
+                mode_send[layer * MODES + k, r : r + 1, :] = kept_rows[r * MODES + k : r * MODES + k + 1]
+                mode_send[layer * MODES + k, 4 + r : 5 + r, :] = padded[r * MODES + k : r * MODES + k + 1]
         wide = jnp.where(own, exact(cot, spec_ref[layer], 1, 1), 0.0)
         kept = wide[:, :D]
         for k in range(1, MODES):
@@ -872,8 +1075,9 @@
 
     lax.fori_loop(0, steps, fourier_back, 0)
     mix_back(0)
-    turned = dense_rows(0).T
-    proj_back = wide4_weight(doubled(turned))
+    mode_land[mine] = mode_send[mine]
+    spread_to_all(devices, mine, lambda r: mode_send.at[r], mode_land, mode_sends, mode_recvs, True)
+    proj_back = wide4_weight(doubled(turned_ref[:, :D]))
 
     def project_back(index, _):
         where = block(index)
@@ -890,6 +1094,13 @@
         return 0
 
     lax.fori_loop(0, steps, project_back, 0)
+    spread_to_all(devices, mine, lambda r: mode_send.at[r], mode_land, mode_sends, mode_recvs, False)
+    landed = mode_land[...].reshape(devices * 8, D)
+    shifted = above(landed[4:], landed[:4])
+    row = lax.broadcasted_iota(jnp.int32, landed.shape, 0)
+    product = exact(jnp.where(lax.rem(row, 8) < 4, landed, 0.0), shifted[:, :FREQ], 0, 0)
+    mode_out[mode_route.area(mode_route.own, FREQ), :] = beside(product[:FREQ], product[FREQ:])
+    mode_route.start(4)
 
     def feed_back(layer, index, cot):
         where = block(index)
@@ -904,6 +1115,12 @@
         return split, halves(inner)
 
     def layer_one_back(index, _):
+        for number, stage in ((2, 4), (4, 5), (6, 6)):
+
+            @pl.when(index == number)
+            def _():
+                mode_route.step(stage)
+
         where = block(index)
         cot = d_keep[where, :]
         _, (high, low) = feed_back(1, index, cot)
@@ -930,7 +1147,8 @@
             plain, summary, mixed = small_keep[layer, s, 0], small_keep[layer, s, 1], small_keep[layer, s, 2]
             turned = exact(query, products[s], 0, 0)
             outer_grad += exact(summary, turned, 0, 0)
-            query_grad += exact(products[s], mixed, 1, 1)
+            if layer:
+                query_grad += exact(products[s], mixed, 1, 1)
             cot = jnp.where(blocks, exact(turned, outer, 1, 1), 0.0)
             both = cot * plain
             key_total += jnp.sum(both * value_gain, 1, keepdims=True)
@@ -938,10 +1156,28 @@
             scaled = key_column * cot * value_gain * (1.0 / points)
             t_keep[s, 0] = tall4_weight(scaled.T)
             t_keep[s, 1] = tall4_weight(scaled)
-        g_attn[layer, :, :D] = query_grad
-        g_attn[layer, :, 3 * D :] = outer_grad
+        if layer:
+            early[5 * D + FREQ : 6 * D + FREQ, :] = query_grad
+            early[6 * D + FREQ : 7 * D + FREQ, :] = outer_grad
+        else:
+            late[6 * D : 7 * D, :] = outer_grad
         return jnp.sum(eye * key_total, 0, keepdims=True), value_total
 
+    mode_route.finish(7)
+    for i in range(2):
+        half = slice(i * D, (i + 1) * D)
+        early[i * D : (i + 1) * D, :] = w1_acc[:D, half] + w1_acc[D:, half]
+        early[(2 + i) * D : (3 + i) * D, :] = w2_acc[1, :D, half] + w2_acc[1, D:, half]
+    sums = p_acc[...]
+    sums = fold(sums[: 2 * D] + sums[2 * D :])
+    early[4 * D : 4 * D + FREQ, :] = (sums[:D, :FREQ] + sums[D:, FREQ:]).T
+    squares = []
+    for part in range(3):
+        sums = quarters(sq_acc[part])
+        squares.append((sums[:FREQ, :FREQ] + sums[FREQ:, FREQ:]).T)
+    early[4 * D + FREQ : 5 * D, :] = beside(squares[0], squares[1])
+    early[5 * D : 5 * D + FREQ, :] = beside(squares[2], jnp.zeros_like(squares[2]))
+    early[7 * D + FREQ :, :] = jnp.zeros((D // 2, D), F32)
     gains = [None, None]
     gains[1] = attend_back(1, [quarters(y_acc[s]) for s in range(count)])
 
@@ -953,7 +1189,15 @@
         mean = dot(beside(*halves(key_cot * key)), mean_weight) * (HEADS / D)
         return beside(scale[:, :D] * (key_cot - key * mean), scale[:, D:] * (value_cot - value * mean))
 
+    early_route.start(0)
+
     def middle_back(index, _):
+        for number in range(1, 8):
+
+            @pl.when(index == number)
+            def _():
+                early_route.step(number - 1)
+
         where = block(index)
         s = index // steps
         cot = norm_back(index, x_keep[where, :], r_keep[where, :])
@@ -969,6 +1213,7 @@
         return 0
 
     lax.fori_loop(0, rows_all, middle_back, 0)
+    early_route.finish(7)
 
     def lift_sum(value):
         value = fold(value)
@@ -983,7 +1228,45 @@
     value_rows = [lift_sum(v_acc[s]) + exact(inner_rows[s], ffn_ref[0, 0], 1, 1) for s in range(count)]
     gains[0] = attend_back(0, [exact(lift_rows, value_rows[s], 0, 0) for s in range(count)])
 
+    query_rows = jnp.zeros((8, D), F32)
+    lift_part = jnp.zeros((8, D), F32)
+    inner_grad = jnp.zeros((D, FF), F32)
+    for s in range(count):
+        query_rows += exact(value_rows[s], small_keep[0, s, 2], 1, 1)
+        lift_part += value_rows[s] + exact(value_rows[s], n_keep[0, s], 1, 1)
+        inner_grad += exact(mid_rows[s], inner_rows[s], 0, 0)
+    for i in range(2):
+        half = slice(i * D, (i + 1) * D)
+        late[i * D : (i + 1) * D, :] = exact(kv_acc[:D, half] + kv_acc[D:, half], centre)
+        late[(2 + i) * D : (3 + i) * D, :] = w2_acc[0, :D, half] + w2_acc[0, D:, half]
+        late[(4 + i) * D : (5 + i) * D, :] = inner_grad[:, half]
+
+    def bias(slot, width=D):
+        return jnp.sum(b_acc[slot * 8 : slot * 8 + 8, :width], 0, keepdims=True)
+
+    rows = [jnp.zeros((3, D), F32)]
+    for layer in range(LAYERS):
+        inner = bias(8 + 2 * layer, FF)
+        rows += [gains[layer][0], gains[layer][1], inner[:, :D], inner[:, D:], bias(7 + 2 * layer)]
+    short = [fold(bias(slot)) for slot in (6, 5, 4, 3, 2)]
+    rows += [beside(short[0], short[1]), beside(short[2], short[3]), beside(short[4], jnp.zeros((1, FREQ), F32))]
+    late[7 * D : 7 * D + 16, :] = above(*rows)
+    lanes = lax.broadcasted_iota(jnp.int32, (1, D), 1)
+    first = jnp.where(lax.rem(lanes, FREQ) == 0, bias(0), 0.0)
+    second = jnp.where(lax.rem(lanes, FREQ) == 0, bias(1), 0.0)
+    late[7 * D + 16 : 7 * D + 24, :] = above(first, second, jnp.zeros((6, D), F32))
+    late[7 * D + 24 : 7 * D + 32, :] = query_rows
+    late[7 * D + 32 : 7 * D + 40, :] = lift_part
+    late[7 * D + 40 :, :] = jnp.zeros((D - 40, D), F32)
+    late_route.start(0)
+
     def front_back(index, _):
+        for number, stage in ((3, 0), (6, 1)):
+
+            @pl.when(index == number)
+            def _():
+                late_route.step(stage)
+
         centred = dot(lifted[block(index), :], w0_kv[...])
         scale = head_scale(centred)
         cot = norm_back(index, centred * scale, scale)
@@ -991,44 +1274,22 @@
         return 0
 
     lax.fori_loop(0, rows_all, front_back, 0)
-
     turned = lift_sum(vt_acc[...])
-    lift_grad = exact(turned, cent_keep[0], 1, 1)
-    for s in range(count):
-        lift_grad += value_rows[s] + exact(value_rows[s], n_keep[0, s], 1, 1)
-    joined = [exact(lift_rows, turned, 0, 0), kv_acc[:D, :] + kv_acc[D:, :]]
-    for layer in range(LAYERS):
-        g_attn[layer, :, D : 2 * D] = exact(joined[layer][:, :D], centre)
-        g_attn[layer, :, 2 * D : 3 * D] = exact(joined[layer][:, D:], centre)
-        g_ffn[layer, 1] = w2_acc[layer, :D, :] + w2_acc[layer, D:, :]
-
-    first = exact(mid_rows[0], inner_rows[0], 0, 0)
-    for s in range(1, count):
-        first += exact(mid_rows[s], inner_rows[s], 0, 0)
-    g_ffn[0, 0] = first
-    g_ffn[1, 0] = w1_acc[:D, :] + w1_acc[D:, :]
-    sums = p_acc[...]
-    sums = fold(sums[: 2 * D] + sums[2 * D :])
-    g_dense[:D, :] = sums[:D, :FREQ] + sums[D:, FREQ:]
-    for part in range(3):
-        sums = quarters(sq_acc[part])
-        start = D + part * FREQ
-        g_dense[start : start + FREQ, :] = sums[:FREQ, :FREQ] + sums[FREQ:, FREQ:]
-
-    def bias(slot, width=D):
-        return jnp.sum(b_acc[slot * 8 : slot * 8 + 8, :width], 0, keepdims=True)
-
-    rows = [lift_grad[0:1], lift_grad[1:2], lift_grad[2:3]]
-    for layer in range(LAYERS):
-        inner = bias(8 + 2 * layer, FF)
-        rows += [gains[layer][0], gains[layer][1], inner[:, :D], inner[:, D:], bias(7 + 2 * layer)]
-    short = [fold(bias(slot)) for slot in (6, 5, 4, 3, 2)]
-    rows += [beside(short[0], short[1]), beside(short[2], short[3]), beside(short[4], jnp.zeros((1, FREQ), F32))]
-    g_vec[...] = above(*rows)
-    lanes = lax.broadcasted_iota(jnp.int32, (1, D), 1)
-    first = jnp.where(lax.rem(lanes, FREQ) == 0, bias(0), 0.0)
-    second = jnp.where(lax.rem(lanes, FREQ) == 0, bias(1), 0.0)
-    g_loss[...] = above(first, second, jnp.zeros((6, D), F32))
+    tail_send[...] = above(turned[:4, :D], turned[:4, D:])
+    tail_land[mine] = tail_send[...]
+    spread_to_all(devices, mine, lambda r: tail_send, tail_land, tail_sends, tail_recvs, True)
+    for stage in range(2, 7):
+        late_route.step(stage)
+    late_route.finish(7)
+    spread_to_all(devices, mine, lambda r: tail_send, tail_land, tail_sends, tail_recvs, False)
+    summed = jnp.sum(tail_land[...], 0)
+    zero = jnp.zeros((4, 2 * D), F32)
+    turned = above(beside(summed[:4], summed[4:]), zero)
+    joined = exact(lift_rows, turned, 0, 0)
+    tail_out[:D, :] = exact(lift_rows, late_out[7 * D + 24 : 7 * D + 32, :], 0, 0)
+    tail_out[D : 2 * D, :] = exact(joined[:, :D], centre)
+    tail_out[2 * D : 3 * D, :] = exact(joined[:, D:], centre)
+    tail_out[3 * D :, :] = late_out[7 * D + 32 : 7 * D + 40, :] + exact(turned, cent_keep[0], 1, 1)
 
 
 def tables(points):
@@ -1046,12 +1307,28 @@
     return np.ascontiguousarray(column), np.ascontiguousarray(row)
 
 
-def local_grads(inputs, attn_w, ffn_w, spec_w, dense_w, vec):
-    count, _, points = inputs.shape
+def summed_grads(samples_in, target, mask, attn_w, ffn_w, spec_w, turned_w, vectors):
+    parts = samples_in.shape[0] // 2
+    count, points = 2, samples_in.shape[2] * parts
+    devices = FLAYERS * MODES
     total = count * points
     steps = points // ROWS
     column, row = tables(points)
     vmem = pl.BlockSpec(memory_space=pltpu.VMEM)
+    first = [
+        ((parts, 8, samples_in.shape[2]), F32),
+        ((parts, 8, samples_in.shape[2]), F32),
+        ((NVEC_ROWS, D), F32),
+        ((8 * D, D), F32),
+        ((8 * D, D), F32),
+        ((8 * D, D), F32),
+        ((8 * D, D), F32),
+        ((devices, 8, D), F32),
+        ((devices, 8, D), F32),
+        ((8, D), F32),
+        ((devices, 8, D), F32),
+    ]
+    numbers = (36, 36, parts - 1, parts - 1, devices - 1, devices - 1, devices - 1, devices - 1)
     scratch = [
         ((total, D), BF16),
         ((total // ROWS, 16, ROWS), BF16),
@@ -1098,43 +1375,239 @@
         ((count, 2, 2 * D, 2 * D), BF16),
         ((count, 4 * D, 2 * D), BF16),
     ]
-    shapes = [attn_w.shape, ffn_w.shape, spec_w.shape, dense_w.shape, vec.shape, (8, D)]
+    shapes = [(8 * D, D), (8 * D, D), (devices * FREQ, D), (3 * D + 8, D)]
     return pl.pallas_call(
-        local_kernel,
+        step_kernel,
         out_shape=[jax.ShapeDtypeStruct(shape, F32) for shape in shapes],
-        in_specs=[vmem] * 8,
-        out_specs=[vmem] * 6,
-        scratch_shapes=[pltpu.VMEM(*item) for item in scratch],
-        compiler_params=pltpu.CompilerParams(vmem_limit_bytes=64 * 2**20 - 2**17),
-    )(inputs, attn_w, ffn_w, spec_w, dense_w, vec, jnp.asarray(column), jnp.asarray(row))
+        in_specs=[vmem] * 10,
+        out_specs=[vmem] * 4,
+        scratch_shapes=[pltpu.VMEM(*item) for item in first]
+        + [pltpu.SemaphoreType.DMA((number,)) for number in numbers]
+        + [pltpu.VMEM(*item) for item in scratch],
+        compiler_params=pltpu.CompilerParams(
+            vmem_limit_bytes=64 * 2**20 - 2**17, collective_id=0, has_side_effects=True
+        ),
+    )(
+        samples_in,
+        target,
+        mask,
+        attn_w,
+        ffn_w,
+        spec_w,
+        turned_w,
+        vectors,
+        jnp.asarray(column),
+        jnp.asarray(row),
+    )
+
+
+def update_kernel(
+    early,
+    late,
+    modes,
+    tail,
+    vectors,
+    vector_m,
+    vector_v,
+    attn_w,
+    ffn_w,
+    spec_w,
+    turned_w,
+    attn_m,
+    ffn_m,
+    spec_m,
+    turned_m,
+    attn_v,
+    ffn_v,
+    spec_v,
+    turned_v,
+    loss_out,
+    count_out,
+    weight_out,
+    update_out,
+    ratio_out,
+    vector_m_out,
+    vector_v_out,
+    vector_w_out,
+    vector_low_out,
+    *rest,
+):
+    outs, scratch = rest[:16], rest[16:]
+    ins = (attn_w, ffn_w, spec_w, turned_w, attn_m, ffn_m, spec_m, turned_m, attn_v, ffn_v, spec_v, turned_v)
+    held, fresh = scratch[:12], scratch[12:28]
+    flat, in_sems, out_sems = scratch[28:]
+
+    blocks = [(2, 0), (2, 1), (1, 1), (0, 1), (0, 0), (1, 0), (3, None)]
+
+    def view(ref, part):
+        return ref if part is None else ref.at[part]
+
+    def load(slot, kind):
+        array, part = blocks[slot]
+        number = kind * 4 + array
+        return pltpu.make_async_copy(
+            view(ins[number], part), view(held[number], part), in_sems.at[slot * 3 + kind]
+        )
+
+    def store(slot, kind):
+        array, part = blocks[slot]
+        number = kind * 4 + array
+        return pltpu.make_async_copy(
+            view(fresh[number], part), view(outs[number], part), out_sems.at[slot * 4 + kind]
+        )
+
+    for slot in range(len(blocks)):
+        for kind in range(3):
+            load(slot, kind).start()
+    misc = late[7 * D + 16 : 7 * D + 24, :]
+    loss_out[0] = jnp.sum(misc[0:1])
+    valid = jnp.sum(misc[1:2], keepdims=True)
+    count_out[0] = jnp.sum(misc[1:2])
+    scale = 1.0 / valid
+
+    def moved(weight, grad, first, second):
+        first_new = BETA_ONE * first + (1.0 - BETA_ONE) * grad
+        second_new = BETA_TWO * second + (1.0 - BETA_TWO) * grad * grad
+        update = (
+            first_new
+            / (1.0 - BETA_ONE**STEP)
+            / (jnp.sqrt(second_new / (1.0 - BETA_TWO**STEP)) + ADAM_EPS)
+            + DECAY * weight
+        )
+        return first_new, second_new, update
+
+    def note(slot, weight_sum, update_sum):
+        weight_norm, update_norm = jnp.sqrt(weight_sum), jnp.sqrt(update_sum)
+        ratio = weight_norm / (update_norm + ADAM_EPS)
+        weight_out[slot] = weight_norm[0, 0]
+        update_out[slot] = update_norm[0, 0]
+        ratio_out[slot] = ratio[0, 0]
+        return RATE * ratio
+
+    def total(value):
+        return jnp.sum(column_sum(value), keepdims=True)
+
+    for i in range(NVEC_ROWS):
+        start = i * D
+        size = min(D, flat.shape[0] - start)
+        row = tail[3 * D + i : 3 * D + i + 1, :] if i < 3 else late[7 * D + i : 7 * D + i + 1, :]
+        flat[start : start + size] = (row * scale)[:, :size].reshape(size)
+    weight = vectors[...]
+    first_new, second_new, update = moved(weight, flat[...], vector_m[...], vector_v[...])
+    vector_m_out[...] = first_new
+    vector_v_out[...] = second_new
+    rate = note(
+        7,
+        jnp.sum(weight * weight).reshape(1, 1),
+        jnp.sum(update * update).reshape(1, 1),
+    )
+    flat[...] = jnp.broadcast_to(rate, (1, D)).reshape(D)[0] * update
+    weight = weight - flat[...]
+    vector_w_out[...] = weight
+    vector_low_out[...] = weight.astype(BF16)
+
+    def grad_blocks(array, part):
+        if array == 0:
+            if part:
+                places = [(early, 5 * D + FREQ), (late, 0), (late, D), (early, 6 * D + FREQ)]
+            else:
+                places = [(tail, 0), (tail, D), (tail, 2 * D), (late, 6 * D)]
+            return [
+                (ref, start, D, 0, (slice(None), slice(j * D, (j + 1) * D)))
+                for j, (ref, start) in enumerate(places)
+            ]
+        if array == 1:
+            ref, starts = (early, (0, 1, 2, 3)) if part else (late, (4, 5, 2, 3))
+            return [
+                (ref, starts[j] * D, D, 0, (j // 2, slice(None), slice(j % 2 * D, j % 2 * D + D)))
+                for j in range(4)
+            ]
+        if array == 3:
+            return [
+                (early, 4 * D, FREQ, 0, (slice(None), slice(0, D))),
+                (early, 4 * D + FREQ, FREQ, 0, (slice(None), slice(D, 2 * D))),
+                (early, 5 * D, FREQ, 0, (slice(None), slice(2 * D, 2 * D + FREQ))),
+            ]
+        return [
+            (modes, (part * MODES + k) * FREQ, FREQ, j * FREQ, (k, j))
+            for k in range(MODES)
+            for j in range(2)
+        ]
+
+    for slot, (array, part) in enumerate(blocks):
+        for kind in range(3):
+            load(slot, kind).wait()
+        weight_ref, first_ref, second_ref = [view(held[kind * 4 + array], part) for kind in range(3)]
+        first_out, second_out, weight_new, low_out = [view(fresh[kind * 4 + array], part) for kind in range(4)]
+        weight_sum = jnp.zeros((1, 1), F32)
+        update_sum = jnp.zeros((1, 1), F32)
+        pieces = grad_blocks(array, part)
+        for ref, start, rows, lane, where in pieces:
+            weight = weight_ref[where]
+            width = weight.shape[1]
+            grad = ref[start : start + rows, lane : lane + width] * scale
+            first_new, second_new, update = moved(weight, grad, first_ref[where], second_ref[where])
+            first_out[where] = first_new
+            second_out[where] = second_new
+            weight_new[where] = update
+            weight_sum += total(weight * weight)
+            update_sum += total(update * update)
+        store(slot, 0).start()
+        store(slot, 1).start()
+        place = (0 + part if array == 0 else 2 + part if array == 1 else 4 + part) if part is not None else 6
+        rate = note(place, weight_sum, update_sum)
+        for ref, start, rows, lane, where in pieces:
+            weight = weight_ref[where] - rate * weight_new[where]
+            weight_new[where] = weight
+            low_out[where] = weight.astype(BF16)
+        store(slot, 2).start()
+        store(slot, 3).start()
+    for slot in range(len(blocks)):
+        for kind in range(4):
+            store(slot, kind).wait()
 
 
 def fast_body(samples_in, target, mask, attn_w, ffn_w, spec_w, dense_w, vectors, *moments):
-    packed = jnp.concatenate([samples_in, target[:, None], mask.astype(F32)[:, None]], 1)
-    whole = lax.all_to_all(packed, "pts", split_axis=0, concat_axis=2, tiled=True)
-    vec = jnp.pad(vectors, (0, -vectors.shape[0] % D)).reshape(-1, D)
-    pieces = local_grads(
-        whole, attn_w, ffn_w, spec_w.reshape(FLAYERS, MODES * 2 * FREQ, FREQ), dense_w, vec
-    )
-    summed = lax.psum(tuple(pieces), ("dp", "pts"))
-    loss_sum, valid_count = jnp.sum(summed[5][0]), jnp.sum(summed[5][1])
-    grads = (
-        summed[0],
-        summed[1],
-        summed[2].reshape(spec_w.shape),
-        summed[3],
-        summed[4].reshape(-1)[: vectors.shape[0]],
-    )
-    grads = tuple(grad * (1.0 / valid_count) for grad in grads)
-    params = (attn_w, ffn_w, spec_w, dense_w, vectors)
-    return tuple(finish(loss_sum, valid_count, params, grads, moments[:5], moments[5:]))
+    flat_spec = spec_w.reshape(FLAYERS, MODES * 2 * FREQ, FREQ)
+    grads = summed_grads(samples_in, target, mask, attn_w, ffn_w, flat_spec, dense_w.T, vectors)
+    sets = [
+        (attn_w, ffn_w, spec_w, dense_w.T),
+        (moments[0], moments[1], moments[2], moments[3].T),
+        (moments[5], moments[6], moments[7], moments[8].T),
+    ]
+    vmem = pl.BlockSpec(memory_space=pltpu.VMEM)
+    smem = pl.BlockSpec(memory_space=pltpu.SMEM)
+    anywhere = pl.BlockSpec(memory_space=pl.ANY)
+    shapes = [item.shape for item in sets[0]]
+    kinds = (F32, F32, F32, BF16)
+    scalar = [jax.ShapeDtypeStruct((1,), F32)] * 2 + [jax.ShapeDtypeStruct((8,), F32)] * 3
+    line = [jax.ShapeDtypeStruct(vectors.shape, kind) for kind in kinds]
+    arrays = [jax.ShapeDtypeStruct(shape, kind) for kind in kinds for shape in shapes]
+    out = pl.pallas_call(
+        update_kernel,
+        out_shape=scalar + line + arrays,
+        in_specs=[vmem] * 7 + [anywhere] * 12,
+        out_specs=[smem] * 5 + [vmem] * 4 + [anywhere] * 16,
+        scratch_shapes=[pltpu.VMEM(shape, F32) for _ in range(3) for shape in shapes]
+        + [pltpu.VMEM(shape, kind) for kind in kinds for shape in shapes]
+        + [pltpu.VMEM(vectors.shape, F32), pltpu.SemaphoreType.DMA((21,)), pltpu.SemaphoreType.DMA((28,))],
+        compiler_params=pltpu.CompilerParams(vmem_limit_bytes=60 * 2**20),
+    )(*grads, vectors, moments[4], moments[9], *sets[0], *sets[1], *sets[2])
+    loss_sum, valid_count, weight_norms, update_norms, ratios = out[:5]
+    line, arrays = out[5:9], out[9:]
+    results = [loss_sum.reshape(()), valid_count.reshape(())]
+    for array in range(4):
+        for kind in range(4):
+            item = arrays[kind * 4 + array]
+            results.append(item.T if array == 3 else item)
+    return tuple(results + list(line) + [weight_norms, update_norms, ratios])
 
 
 def choose_body(*arrays):
     samples_in = arrays[0]
-    parts = lax.axis_size("pts")
-    regular = samples_in.shape[0] == 2 * parts and samples_in.shape[2] * parts % ROWS == 0
-    return (fast_body if regular else body)(*arrays)
+    dp, parts = lax.axis_size("dp"), lax.axis_size("pts")
+    fits = dp * parts == FLAYERS * MODES and dp == 4 and samples_in.shape[0] == 2 * parts
+    return (fast_body if fits and samples_in.shape[2] * parts % ROWS == 0 else body)(*arrays)
 
 
 def solution(mesh):

time: 285 us -> 157 us (0.55)
  waiting for transfers between devices: 96.4 us -> 0 us
  Pallas kernels: 91.2 us -> 156 us
  blocking collectives: 38.9 us -> 0 us
  other arithmetic: 21.7 us -> 0 us
  between operations: 18 us -> 0.86 us
  local copies, waits for them, and re-layouts: 10.3 us -> 0 us
  starting transfers between devices: 7.32 us -> 0 us
    psum x1 -> x0, waiting for transfers between devices: 92.5 us -> none  [fast_body(): summed = lax.psum(tuple(pieces), ('dp', 'pts'))]
    pallas_call x1 -> x2, Pallas kernels: 91.2 us -> 156 us  [the longest x1 144 us: summed_grads(): pl.pallas_call(step_kernel, out_shape=[jax.ShapeDtypeStruct(shape, F32) f...]
    psum x1 -> x0, blocking collectives: 38.9 us -> none  [fast_body(): summed = lax.psum(tuple(pieces), ('dp', 'pts'))]
    reduce_sum x7 -> x0, other arithmetic: 9.97 us -> none  [the longest x4 7.08 us: trust_step(): weight_norm = jnp.sqrt(jnp.sum(weight * weight, axes))]
    all_to_all x1 -> x0, starting transfers between devices: 7.28 us -> none  [fast_body(): lax.all_to_all(packed, 'pts', split_axis=0, concat_axis=2, tiled=True)]
    convert_element_type x5 -> x0, other arithmetic: 6.33 us -> none  [finish(): fresh.astype(jnp.bfloat16)]
    unnamed x59 -> x0, local copies, waits for them, and re-layouts: 5.78 us -> none
    all_to_all x1 -> x0, waiting for transfers between devices: 3.88 us -> none  [fast_body(): lax.all_to_all(packed, 'pts', split_axis=0, concat_axis=2, tiled=True)]
  transfers between devices with their start and end apart: 2 -> 0, of which waited for: 2 -> 0; matrix products, arithmetic and copies ran while one was open for 2% -> 0% of each run, Pallas kernels for 0% -> 0%
where the time goes in v2:
time: 157 us
  Pallas kernels  156 us (99%)
    pallas_call x1, Pallas kernels, summed_grads(): pl.pallas_call(step_kernel, out_shape=[jax.ShapeDtypeStruct(shape, F32) f...  144 us
    pallas_call x1, Pallas kernels, fast_body(): pl.pallas_call(update_kernel, out_shape=scalar + line + arrays, in_specs=...  11.7 us

profile of v2, /device:TPU:0, one launch (start us, length us, event | category | flops | bytes accessed | tf_op | source)
XLA Modules:
  0.0 156.9 jit_solution(17215307529073186793)
XLA Ops:
  0.7 144.4 %shard_map.387 = (f32[1024,128]{1,0:T(8,128)}, f32[1024,128]{1,0:T(8,128)}, f32[2048,128]{1,0:T(8,128)}, f32[392,128]{1,0:T(8,128)}) custom-call(f32[16,2,256]{2,1,0:T(2,128)} %samples_ref.1, f32[16,256]{1,0:T(8,128)} %target_ref.1, s32[16,256]{1,0:T(8,128)} %mask_ref.1, f32[2,128,512]{2,1,0:T(8,128)} %attn_w.1, f32[2,2,128,256]{3,2,1,0:T(8,128)} %ffn_w.1, ...), custom_call_target="tpu_custom_call" | custom-call | tf_op jit(solution)/shard_map/pallas_call | solution.py:1379
  145.0 11.7 %shard_map.388 = (f32[1]{0:T(128)}, f32[1]{0:T(128)}, f32[8]{0:T(128)}, f32[8]{0:T(128)}, f32[8]{0:T(128)}, /*index=5*/f32[1984]{0:T(1024)}, f32[1984]{0:T(1024)...) custom-call(f32[1024,128]{1,0:T(8,128)} %get-tuple-element.54.early,, ...), custom_call_target="tpu_custom_call" | custom-call | tf_op jit(solution)/shard_map/pallas_call | solution.py:1586

commit v3 on v2

--- a/solution.py
+++ b/solution.py
@@ -353,7 +353,7 @@
 
 F32 = jnp.float32
 BF16 = jnp.bfloat16
-ROWS = 512
+ROWS = 1024
 NVEC_ROWS = 16
 
 
@@ -431,26 +431,6 @@
     return fold(dot(beside(high, middle), weights[0])) + dot(beside(high, low), weights[1])
 
 
-def wide4_weight(weight):
-    high, low = halves(weight)
-    return above(high, high, low, low)
-
-
-def wide4(pieces, weight):
-    high, low = pieces
-    return dot(beside(high, low, high, low), weight)
-
-
-def tall4_weight(weight):
-    high, low = halves(weight)
-    pair = beside(high, low)
-    return above(pair, pair)
-
-
-def tall4(pieces, weight):
-    return fold(dot(beside(*pieces), weight))
-
-
 def head_blocks(width):
     row = lax.broadcasted_iota(jnp.int32, (width, width), 0)
     column = lax.broadcasted_iota(jnp.int32, (width, width), 1)
@@ -485,27 +465,13 @@
 class Route:
     def __init__(self, rows, full, flat, landing, sends, receives, first):
         x, core, z, y = position()
-        a = (1 - core) * x + core * y
-        b = (1 - core) * y + core * x
-        self.keep = (core, a, b, z)
+        self.core, self.group = core, FLAYERS * MODES // 2
+        self.place = 8 * ((1 - core) * x + core * y) + 4 * ((1 - core) * y + core * x) + z
         self.rows, self.full, self.flat, self.landing = rows, full, flat, landing
         self.sends, self.receives, self.first = sends, receives, first
-        self.peers = [
-            device_of(x, 1 - core, z, y),
-            device_of(x + (1 - core) * (1 - 2 * x), core, z, y + core * (1 - 2 * y)),
-            device_of(x + core * (1 - 2 * x), core, z, y + (1 - core) * (1 - 2 * y)),
-        ]
-        self.far = [device_of(x, core, (z + k) % 4, y) for k in (1, 2, 3)]
-        half, quarter, eighth, least = rows // 2, rows // 4, rows // 8, rows // 32
-        self.least = least
-        self.sizes = [half, quarter, eighth]
-        self.starts = [core * half, core * half + a * quarter, core * half + a * quarter + b * eighth]
-        self.own = self.starts[2] + z * least
-        self.others = [
-            (1 - core) * half,
-            core * half + (1 - a) * quarter,
-            core * half + a * quarter + (1 - b) * eighth,
-        ]
+        self.peer = device_of(x, 1 - core, z, y)
+        self.half, self.least = rows // 2, rows // (2 * self.group)
+        self.own = core * self.half + self.place * self.least
 
     def area(self, start, size):
         return pl.ds(pl.multiple_of(start, self.least), size)
@@ -520,50 +486,54 @@
             device_id_type=MESH,
         )
 
-    def copies(self, stage, receiving=False):
-        z = self.keep[3]
-        if stage < 3:
-            place = self.landing.at[pl.ds(self.rows - 2 * self.sizes[stage], self.sizes[stage])]
-            source = self.flat.at[self.area(self.others[stage], self.sizes[stage])]
-            return [self.link(source, place, stage, self.peers[stage])]
-        if stage == 3:
-            found = []
-            for k in (1, 2, 3):
-                start = self.starts[2] + (z + k) % 4 * self.least
-                place = self.landing.at[pl.ds(self.rows - self.sizes[2] + (k - 1) * self.least, self.least)]
-                found.append(self.link(self.flat.at[self.area(start, self.least)], place, 2 + k, self.far[k - 1]))
-            return found
-        if stage == 4:
-            piece = self.full.at[self.area(self.own, self.least)]
-            found = []
-            for k in (1, 2, 3):
-                start = self.starts[2] + (z + 4 - k) % 4 * self.least if receiving else self.own
-                found.append(self.link(piece, self.full.at[self.area(start, self.least)], 5 + k, self.far[k - 1]))
-            return found
-        level = 7 - stage
-        size = self.sizes[level]
-        piece = self.full.at[self.area(self.starts[level], size)]
-        target = self.full.at[self.area(self.others[level], size)] if receiving else piece
-        return [self.link(piece, target, 4 + stage, self.peers[level])]
+    def each(self, stage, start):
+        half, least, core, group = self.half, self.least, self.core, self.group
+        if stage in (0, 3):
+            if stage:
+                source = self.full.at[self.area(core * half, half)]
+                target = source if start else self.full.at[self.area((1 - core) * half, half)]
+            else:
+                source, target = self.flat.at[self.area((1 - core) * half, half)], self.landing.at[pl.ds(0, half)]
+            copy = self.link(source, target, 2 * group - 2 if stage else 2 * group - 1, self.peer)
+            if start:
+                copy.start()
+            else:
+                copy.wait()
+            return
+
+        def one(i, _):
+            other = lax.rem(self.place + 1 + i, group)
+            sender = lax.rem(self.place + group - 1 - i, group)
+            if stage == 1:
+                source = self.flat.at[self.area(core * half + other * least, least)]
+                target = self.landing.at[self.area(half + i * least, least)]
+            else:
+                source = self.full.at[self.area(self.own, least)]
+                target = source if start else self.full.at[self.area(core * half + sender * least, least)]
+            copy = self.link(source, target, (stage - 1) * (group - 1) + i, device_at(core * group + other))
+            if start:
+                copy.start()
+            else:
+                copy.wait()
+            return 0
+
+        lax.fori_loop(0, group - 1, one, 0)
 
     def start(self, stage):
-        if stage == 4 and self.flat is not None:
+        if stage == 2 and self.flat is not None:
             self.full[self.area(self.own, self.least), :] = self.flat[self.area(self.own, self.least), :]
-        for copy in self.copies(stage):
-            copy.start()
+        self.each(stage, True)
 
     def finish(self, stage):
-        for copy in self.copies(stage, True):
-            copy.wait()
-        if stage < 3:
-            mine = self.area(self.starts[stage], self.sizes[stage])
-            place = pl.ds(self.rows - 2 * self.sizes[stage], self.sizes[stage])
-            self.flat[mine, :] += self.landing[place, :]
-        if stage == 3:
+        self.each(stage, False)
+        if stage == 0:
+            self.flat[self.area(self.core * self.half, self.half), :] += self.landing[: self.half, :]
+        if stage == 1:
             mine = self.area(self.own, self.least)
             total = self.flat[mine, :]
-            for k in range(3):
-                total = total + self.landing[pl.ds(self.rows - self.sizes[2] + k * self.least, self.least), :]
+            for i in range(self.group - 1):
+                start = self.half + i * self.least
+                total = total + self.landing[start : start + self.least, :]
             self.flat[mine, :] = total
 
     def step(self, stage):
@@ -645,7 +615,6 @@
     h1_keep,
     h2_keep,
     z_keep,
-    zs_keep,
     e_keep,
     s_acc,
     w0_kv,
@@ -659,7 +628,6 @@
     stack_ref,
     sq_acc,
     p_acc,
-    y_acc,
     w2_acc,
     w1_acc,
     kv_acc,
@@ -679,8 +647,8 @@
     pts = 2 * z + y
     mine = 16 * core + 8 * ((1 - core) * x + core * y) + 4 * ((1 - core) * y + core * x) + z
     early_route = Route(early.shape[0], early_out, early, early_land, route_send, route_recv, 0)
-    late_route = Route(late.shape[0], late_out, late, late_land, route_send, route_recv, 12)
-    mode_route = Route(mode_out.shape[0], mode_out, None, None, route_send, route_recv, 24)
+    late_route = Route(late.shape[0], late_out, late, late_land, route_send, route_recv, devices)
+    mode_route = Route(mode_out.shape[0], mode_out, None, None, route_send, route_recv, 2 * devices)
 
     barrier = pltpu.get_barrier_semaphore()
 
@@ -773,21 +741,24 @@
             w0_kv[...] = lift_weight(exact(lift_rows, keyed))
         else:
             w_kv[...] = wide6_weight(keyed)
-            w_kvt[...] = tall4_weight(keyed.T)
+            pair, rest = tall6_weight(keyed.T)
+            w_kvt[:, : 2 * D] = pair
+            w_kvt[:, 2 * D :] = rest
         first, second = ffn_ref[layer, 0], ffn_ref[layer, 1]
         if layer:
             w_in[...] = wide6_weight(first)
-            w_int[...] = tall4_weight(first.T)
+            pair, rest = tall6_weight(first.T)
+            w_int[:, : 2 * D] = pair
+            w_int[:, 2 * D :] = rest
         pair, rest = tall6_weight(second.T)
         w_out0[layer] = pair
         w_out1[layer] = rest
-        w_outt[layer] = wide4_weight(second)
+        w_outt[layer] = wide6_weight(second)
 
     s_acc[...] = jnp.zeros_like(s_acc)
     coef_acc[...] = jnp.zeros_like(coef_acc)
     sq_acc[...] = jnp.zeros_like(sq_acc)
     p_acc[...] = jnp.zeros_like(p_acc)
-    y_acc[...] = jnp.zeros_like(y_acc)
     w2_acc[...] = jnp.zeros_like(w2_acc)
     w1_acc[...] = jnp.zeros_like(w1_acc)
     kv_acc[...] = jnp.zeros_like(kv_acc)
@@ -828,7 +799,7 @@
             x_keep[where, :] = normal
             r_keep[where, :] = scale
         high, low = halves(normal)
-        s_acc[layer, index // steps] += dot(
+        s_acc[index // steps] += dot(
             beside(high[:, :D], low[:, :D]), beside(high[:, D:], low[:, D:]), 0, 0
         )
 
@@ -846,7 +817,7 @@
         value_gain = vector("value_gain", layer).reshape(1, D)
         key_column = jnp.sum(eye * key_gain, 1, keepdims=True)
         for s in range(count):
-            plain = jnp.where(blocks, quarters(s_acc[layer, s]), 0.0) * (1.0 / points)
+            plain = jnp.where(blocks, quarters(s_acc[s]), 0.0) * (1.0 / points)
             summary = key_column * plain * value_gain
             mixed = exact(summary, weight[:, 3 * D :])
             both = exact(weight[:, :D], mixed)
@@ -863,7 +834,9 @@
                 pair, rest = tall6_weight(both)
                 wz[s, : 2 * D, :] = pair
                 wz[s, 2 * D :, :D] = rest
-                nt_keep[s] = tall4_weight(both.T)
+                pair, rest = tall6_weight(both.T)
+                nt_keep[s, :, : 2 * D] = pair
+                nt_keep[s, :, 2 * D :] = rest
 
     def feed(layer, index, mid, inner):
         where = block(index)
@@ -879,6 +852,7 @@
 
     lax.fori_loop(0, rows_all, front_zero, 0)
     summarise(0)
+    s_acc[...] = jnp.zeros_like(s_acc)
 
     def layer_zero(index, _):
         where = block(index)
@@ -887,12 +861,14 @@
         out = feed(0, index, dot(data, w0_g[s]), dot(data, w0_u[s]))
         d_keep[where, :] = out
         pieces = thirds(out)
-        h1_keep[where, :] = beside(*pieces)
+        h1_keep[where, :] = beside(pieces[0], pieces[1])
+        h2_keep[where, 2 * D :] = pieces[2]
         normalise(1, index, wide6(pieces, w_kv[...]))
         return 0
 
     lax.fori_loop(0, rows_all, layer_zero, 0)
     summarise(1)
+    s_acc[...] = jnp.zeros_like(s_acc)
 
     def pieces_of(ref, where, number=3):
         value = ref[where, : number * D]
@@ -901,7 +877,7 @@
     def layer_one(index, _):
         where = block(index)
         s = index // steps
-        pieces = pieces_of(h1_keep, where)
+        pieces = pieces_of(h1_keep, where, 2) + [h2_keep[where, 2 * D :]]
         mid = d_keep[where, :] + tall6(pieces, (wz[s, : 2 * D, :], wz[s, 2 * D :, :D]))
         pieces = thirds(mid)
         mid_keep[where, :] = beside(pieces[0], pieces[1])
@@ -917,7 +893,7 @@
 
     proj0, proj1 = tall6_weight(doubled(dense_rows(0)))
     locals6 = [tall6_weight(doubled(dense_rows(part))) for part in (1, 2, 3)]
-    locals4 = [tall4_weight(doubled(dense_rows(part).T)) for part in (1, 2, 3)]
+    turned6 = [tall6_weight(doubled(dense_rows(part).T)) for part in (1, 2, 3)]
     own = lax.broadcasted_iota(jnp.int32, (2 * count * MODES, MODES * D), 1) // D == lax.rem(
         lax.broadcasted_iota(jnp.int32, (2 * count * MODES, MODES * D), 0), MODES
     )
@@ -1006,7 +982,7 @@
     def fourier_one(index, _):
         where = block(index)
         field, slope = fourier_field(0, where)
-        zs_keep[where, :] = slope
+        d_keep[where, :] = slope
         pieces = thirds(field)
         z_keep[1, where, :] = beside(*pieces)
         take_coef(index, pieces[0], pieces[1])
@@ -1047,48 +1023,48 @@
         b_acc[16:24, :D] += column_sum(hidden * cot)
         cot = cot * out_row * hidden_slope
         b_acc[24:32, :D] += column_sum(cot)
-        split = halves(cot)
-        sq_acc[2] += pair_product(pieces[:2], split)
-        cot = tall4(split, locals4[2]) * slope
+        split = thirds(cot)
+        sq_acc[2] += pair_product(pieces[:2], split[:2])
+        cot = tall6(split, turned6[2]) * slope
         b_acc[32:40, :D] += column_sum(cot)
-        split = halves(cot)
+        split = thirds(cot)
         e_keep[where, :] = beside(*split)
-        sq_acc[1] += pair_product(pieces_of(z_keep.at[1], where, 2), split)
-        take_coef(index, *split)
+        sq_acc[1] += pair_product(pieces_of(z_keep.at[1], where, 2), split[:2])
+        take_coef(index, *split[:2])
         return 0
 
     lax.fori_loop(0, steps, loss_step, 0)
     mix_back(1)
 
     def fourier_cot(layer, where):
-        return tall4(pieces_of(e_keep, where, 2), locals4[layer]) + dot(table_ref[where, :], stack_ref[...])
+        return tall6(pieces_of(e_keep, where), turned6[layer]) + dot(table_ref[where, :], stack_ref[...])
 
     def fourier_back(index, _):
         where = block(index)
-        cot = fourier_cot(1, where) * zs_keep[where, :]
+        cot = fourier_cot(1, where) * d_keep[where, :]
         b_acc[40:48, :D] += column_sum(cot)
-        split = halves(cot)
+        split = thirds(cot)
         e_keep[where, :] = beside(*split)
-        sq_acc[0] += pair_product(pieces_of(z_keep.at[0], where, 2), split)
-        take_coef(index, *split)
+        sq_acc[0] += pair_product(pieces_of(z_keep.at[0], where, 2), split[:2])
+        take_coef(index, *split[:2])
         return 0
 
     lax.fori_loop(0, steps, fourier_back, 0)
     mix_back(0)
     mode_land[mine] = mode_send[mine]
     spread_to_all(devices, mine, lambda r: mode_send.at[r], mode_land, mode_sends, mode_recvs, True)
-    proj_back = wide4_weight(doubled(turned_ref[:, :D]))
+    proj_back = wide6_weight(doubled(turned_ref[:, :D]))
 
     def project_back(index, _):
         where = block(index)
         later = block(index + steps)
         cot = fourier_cot(0, where)
         b_acc[48:56, :D] += column_sum(cot)
-        split = halves(cot)
+        split = thirds(cot)
         first = pieces_of(h2_keep, where, 2)
         second = pieces_of(h2_keep, later, 2)
-        p_acc[...] += dot(beside(first[0], second[0], first[1], second[1]), beside(*split), 0, 0)
-        rows = wide4(split, proj_back)
+        p_acc[...] += dot(beside(first[0], second[0], first[1], second[1]), beside(*split[:2]), 0, 0)
+        rows = wide6(split, proj_back)
         d_keep[where, :] = rows[:, :D]
         d_keep[later, :] = rows[:, D:]
         return 0
@@ -1100,36 +1076,31 @@
     row = lax.broadcasted_iota(jnp.int32, landed.shape, 0)
     product = exact(jnp.where(lax.rem(row, 8) < 4, landed, 0.0), shifted[:, :FREQ], 0, 0)
     mode_out[mode_route.area(mode_route.own, FREQ), :] = beside(product[:FREQ], product[FREQ:])
-    mode_route.start(4)
+    mode_route.start(2)
 
     def feed_back(layer, index, cot):
         where = block(index)
         base = 56 + layer * 16
         b_acc[base : base + 8, :D] += column_sum(cot)
-        split = halves(cot)
+        split = thirds(cot)
         act = act_keep[layer, where, :]
-        w2_acc[layer] += dot(beside(*split), act[:, :FF], 0, 0)
+        w2_acc[layer] += dot(beside(*split[:2]), act[:, :FF], 0, 0)
         w2_acc[layer, :D, :] += dot(split[0], act[:, FF:], 0, 0)
-        inner = wide4(split, w_outt[layer]) * slope_keep[layer, where, :]
+        inner = wide6(split, w_outt[layer]) * slope_keep[layer, where, :]
         b_acc[base + 8 : base + 16, :] += column_sum(inner)
-        return split, halves(inner)
+        return split, thirds(inner)
 
     def layer_one_back(index, _):
-        for number, stage in ((2, 4), (4, 5), (6, 6)):
-
-            @pl.when(index == number)
-            def _():
-                mode_route.step(stage)
-
         where = block(index)
         cot = d_keep[where, :]
-        _, (high, low) = feed_back(1, index, cot)
+        _, pieces = feed_back(1, index, cot)
+        high, low = pieces[:2]
         mid = mid_keep[where, :]
         w1_acc[...] += dot(mid, high, 0, 0)
         w1_acc[:D, :] += dot(mid[:, :D], low, 0, 0)
-        cot = cot + tall4((high, low), w_int[...])
+        cot = cot + tall6(pieces, (w_int[:, : 2 * D], w_int[:, 2 * D :]))
         d_keep[where, :] = cot
-        y_acc[index // steps] += pair_product(pieces_of(h1_keep, where, 2), halves(cot))
+        s_acc[index // steps] += pair_product(pieces_of(h1_keep, where, 2), halves(cot))
         return 0
 
     lax.fori_loop(0, rows_all, layer_one_back, 0)
@@ -1154,8 +1125,10 @@
             key_total += jnp.sum(both * value_gain, 1, keepdims=True)
             value_total += jnp.sum(both * key_column, 0, keepdims=True)
             scaled = key_column * cot * value_gain * (1.0 / points)
-            t_keep[s, 0] = tall4_weight(scaled.T)
-            t_keep[s, 1] = tall4_weight(scaled)
+            for i, item in enumerate((scaled.T, scaled)):
+                pair, rest = tall6_weight(item)
+                t_keep[s, i, :, : 2 * D] = pair
+                t_keep[s, i, :, 2 * D :] = rest
         if layer:
             early[5 * D + FREQ : 6 * D + FREQ, :] = query_grad
             early[6 * D + FREQ : 7 * D + FREQ, :] = outer_grad
@@ -1163,7 +1136,6 @@
             late[6 * D : 7 * D, :] = outer_grad
         return jnp.sum(eye * key_total, 0, keepdims=True), value_total
 
-    mode_route.finish(7)
     for i in range(2):
         half = slice(i * D, (i + 1) * D)
         early[i * D : (i + 1) * D, :] = w1_acc[:D, half] + w1_acc[D:, half]
@@ -1179,41 +1151,46 @@
     early[5 * D : 5 * D + FREQ, :] = beside(squares[2], jnp.zeros_like(squares[2]))
     early[7 * D + FREQ :, :] = jnp.zeros((D // 2, D), F32)
     gains = [None, None]
-    gains[1] = attend_back(1, [quarters(y_acc[s]) for s in range(count)])
+    gains[1] = attend_back(1, [quarters(s_acc[s]) for s in range(count)])
 
     def norm_back(index, normal, scale):
         s = index // steps
         key, value = normal[:, :D], normal[:, D:]
-        key_cot = tall4(halves(value), t_keep[s, 0])
-        value_cot = tall4(halves(key), t_keep[s, 1])
+        key_cot = tall6(thirds(value), (t_keep[s, 0, :, : 2 * D], t_keep[s, 0, :, 2 * D :]))
+        value_cot = tall6(thirds(key), (t_keep[s, 1, :, : 2 * D], t_keep[s, 1, :, 2 * D :]))
         mean = dot(beside(*halves(key_cot * key)), mean_weight) * (HEADS / D)
         return beside(scale[:, :D] * (key_cot - key * mean), scale[:, D:] * (value_cot - value * mean))
 
     early_route.start(0)
 
     def middle_back(index, _):
-        for number in range(1, 8):
-
-            @pl.when(index == number)
-            def _():
-                early_route.step(number - 1)
+        @pl.when(index == 1)
+        def _():
+            mode_route.step(2)
+            early_route.step(0)
 
         where = block(index)
         s = index // steps
         cot = norm_back(index, x_keep[where, :], r_keep[where, :])
-        high, low = halves(cot)
-        kept = h1_keep[where, : 2 * D]
+        pieces = thirds(cot)
+        high, low = pieces[:2]
+        kept = h1_keep[where, :]
         kv_acc[...] += dot(kept, high, 0, 0)
         kv_acc[:D, :] += dot(kept[:, :D], low, 0, 0)
         out = d_keep[where, :]
-        out = out + tall4(halves(out), nt_keep[s]) + tall4((high, low), w_kvt[...])
+        out = (
+            out
+            + tall6(thirds(out), (nt_keep[s, :, : 2 * D], nt_keep[s, :, 2 * D :]))
+            + tall6(pieces, (w_kvt[:, : 2 * D], w_kvt[:, 2 * D :]))
+        )
         outer, inner = feed_back(0, index, out)
-        v_acc[s] += dot(lrows[index], beside(*outer))
-        u_acc[s] += dot(lrows[index], beside(*inner))
+        v_acc[s] += dot(lrows[index], beside(*outer[:2]))
+        u_acc[s] += dot(lrows[index], beside(*inner[:2]))
         return 0
 
     lax.fori_loop(0, rows_all, middle_back, 0)
-    early_route.finish(7)
+    mode_route.finish(3)
+    early_route.step(1)
 
     def lift_sum(value):
         value = fold(value)
@@ -1261,11 +1238,9 @@
     late_route.start(0)
 
     def front_back(index, _):
-        for number, stage in ((3, 0), (6, 1)):
-
-            @pl.when(index == number)
-            def _():
-                late_route.step(stage)
+        @pl.when(index == 1)
+        def _():
+            late_route.step(0)
 
         centred = dot(lifted[block(index), :], w0_kv[...])
         scale = head_scale(centred)
@@ -1278,10 +1253,12 @@
     tail_send[...] = above(turned[:4, :D], turned[:4, D:])
     tail_land[mine] = tail_send[...]
     spread_to_all(devices, mine, lambda r: tail_send, tail_land, tail_sends, tail_recvs, True)
-    for stage in range(2, 7):
-        late_route.step(stage)
-    late_route.finish(7)
+    early_route.step(2)
+    late_route.step(1)
+    early_route.finish(3)
+    late_route.step(2)
     spread_to_all(devices, mine, lambda r: tail_send, tail_land, tail_sends, tail_recvs, False)
+    late_route.finish(3)
     summed = jnp.sum(tail_land[...], 0)
     zero = jnp.zeros((4, 2 * D), F32)
     turned = above(beside(summed[:4], summed[4:]), zero)
@@ -1328,42 +1305,40 @@
         ((8, D), F32),
         ((devices, 8, D), F32),
     ]
-    numbers = (36, 36, parts - 1, parts - 1, devices - 1, devices - 1, devices - 1, devices - 1)
+    numbers = (3 * devices, 3 * devices, parts - 1, parts - 1, devices - 1, devices - 1, devices - 1, devices - 1)
     scratch = [
         ((total, D), BF16),
         ((total // ROWS, 16, ROWS), BF16),
         ((6 * D, 2 * D), BF16),
-        ((4 * D, 2 * D), BF16),
+        ((4 * D, 3 * D), BF16),
         ((6 * D, FF), BF16),
-        ((2 * FF, 2 * D), BF16),
+        ((2 * FF, 3 * D), BF16),
         ((count, D, FF), BF16),
         ((count, 8, D), F32),
         ((LAYERS, 2 * FF, 2 * D), BF16),
         ((LAYERS, 2 * FF, D), BF16),
-        ((LAYERS, 4 * D, FF), BF16),
+        ((LAYERS, 6 * D, FF), BF16),
         ((total, 2 * D), F32),
         ((total, 2 * D), F32),
         ((LAYERS, total, FF), F32),
         ((LAYERS, total, 2 * FF), BF16),
         ((total, 2 * D), BF16),
-        ((total, 3 * D), BF16),
+        ((total, 2 * D), BF16),
         ((total, 3 * D), BF16),
         ((FLAYERS, points, 3 * D), BF16),
-        ((points, D), F32),
-        ((points, 2 * D), BF16),
-        ((LAYERS, count, 2 * D, 2 * D), F32),
+        ((points, 3 * D), BF16),
+        ((count, 2 * D, 2 * D), F32),
         ((D, 2 * D), BF16),
         ((count, D, D), BF16),
         ((LAYERS, count, D, D), F32),
         ((LAYERS, count, 3, D, D), F32),
-        ((count, 2 * D, 2 * D), BF16),
+        ((count, 2 * D, 3 * D), BF16),
         ((LAYERS, D, 2 * D), F32),
         ((4 * MODES, 2 * D), F32),
         ((FLAYERS, 2 * count * MODES, D), F32),
         ((2 * D, D), BF16),
         ((3, 2 * D, 2 * D), F32),
         ((4 * D, 2 * D), F32),
-        ((count, 2 * D, 2 * D), F32),
         ((LAYERS, 2 * D, FF), F32),
         ((2 * D, FF), F32),
         ((2 * D, 2 * D), F32),
@@ -1372,7 +1347,7 @@
         ((16, 4 * D), F32),
         ((96, FF), F32),
         ((total, D), F32),
-        ((count, 2, 2 * D, 2 * D), BF16),
+        ((count, 2, 2 * D, 3 * D), BF16),
         ((count, 4 * D, 2 * D), BF16),
     ]
     shapes = [(8 * D, D), (8 * D, D), (devices * FREQ, D), (3 * D + 8, D)]

time: 157 us -> 127 us (0.81)
  Pallas kernels: 156 us -> 126 us
    pallas_call x1, Pallas kernels: 144 us -> 114 us  [summed_grads(): pl.pallas_call(step_kernel, out_shape=[jax.ShapeDtypeStruct(shape, F32) f...]
where the time goes in v3:
time: 127 us; the launch traced here: 126 us
  Pallas kernels  126 us (99%)
    pallas_call x1, Pallas kernels, summed_grads(): pl.pallas_call(step_kernel, out_shape=[jax.ShapeDtypeStruct(shape, F32) f...  114 us
    pallas_call x1, Pallas kernels, fast_body(): pl.pallas_call(update_kernel, out_shape=scalar + line + arrays, in_specs=...  11.7 us

profile of v3, /device:TPU:0, one launch (start us, length us, event | category | flops | bytes accessed | tf_op | source)
XLA Modules:
  0.0 126.4 jit_solution(2612506777994651884)
XLA Ops:
  0.7 113.9 %shard_map.387 = (f32[1024,128]{1,0:T(8,128)}, f32[1024,128]{1,0:T(8,128)}, f32[2048,128]{1,0:T(8,128)}, f32[392,128]{1,0:T(8,128)}) custom-call(f32[16,2,256]{2,1,0:T(2,128)} %samples_ref.1, f32[16,256]{1,0:T(8,128)} %target_ref.1, s32[16,256]{1,0:T(8,128)} %mask_ref.1, f32[2,128,512]{2,1,0:T(8,128)} %attn_w.1, f32[2,2,128,256]{3,2,1,0:T(8,128)} %ffn_w.1, ...), custom_call_target="tpu_custom_call" | custom-call | tf_op jit(solution)/shard_map/pallas_call | solution.py:1354
  114.5 11.7 %shard_map.388 = (f32[1]{0:T(128)}, f32[1]{0:T(128)}, f32[8]{0:T(128)}, f32[8]{0:T(128)}, f32[8]{0:T(128)}, /*index=5*/f32[1984]{0:T(1024)}, f32[1984]{0:T(1024)...) custom-call(f32[1024,128]{1,0:T(8,128)} %get-tuple-element.54.early,, ...), custom_call_target="tpu_custom_call" | custom-call | tf_op jit(solution)/shard_map/pallas_call | solution.py:1561
